TPU v7x, 256 devices: a whole 4x4x8 slice. The times are simulated.
256 devices in a mesh: pool: 2 (over y_lo), rank: 128 (over z, x, y_hi, core).
Axes of the slice: x: 4, y: 4 (y_hi: 2, y_lo: 2; y = y_hi * 2 + y_lo), z: 8, core: 2. Of those that a mesh axis runs over, the one named last changes fastest.
Arguments:
- queries: bfloat16 [256, 64, 256], P(('pool', 'rank'))
- cache_keys: bfloat16 [256, 2048, 256], P(('pool', 'rank'))
- cache_values: bfloat16 [256, 2048, 256], P(('pool', 'rank')), may hold values from -6 to 6
- new_keys: bfloat16 [256, 256], P(('pool', 'rank')), may hold values from -6 to 6
- new_values: bfloat16 [256, 256], P(('pool', 'rank')), may hold values from -6 to 6
- lengths: int32 [256], P(('pool', 'rank')), may hold values from 512 to 2048, as said below
- residual: bfloat16 [256, 7168], P('pool', 'rank'), may hold values from -4 to 4
- out_weight: bfloat16 [7168, 16384], P('rank'), may hold values from -0.375 to 0.375
- norm_gain: float32 [7168], replicated, may hold values from 0.5 to 1.5
- router_weight: bfloat16 [7168, 8], replicated, may hold values from -0.0625 to 0.0625
- routes: int32 [256, 3], replicated, may hold values from 0 to 7, all different within a row; in each aligned block of 256 rows (0 to 255, 256 to 511, ...) at most 160 rows name the same one
- gate_tiles: bfloat16 [256, 7168, 160], P(('pool', 'rank')), may hold values from -0.0625 to 0.0625
- up_tiles: bfloat16 [256, 7168, 160], P(('pool', 'rank')), may hold values from -0.0625 to 0.0625
- down_tiles: bfloat16 [256, 160, 7168], P(('pool', 'rank')), may hold values from -0.078125 to 0.078125
Outputs:
- output: bfloat16 [256, 7168], P('pool', 'rank')
Inputs may be any that keep to these rules, and one draw needn't show every extreme that they name: `lengths`: some row's cache is full. `routes`: each row names 3 different experts; over all 256 rows no expert is named by more than 160 rows, a bound that some block reaches.
All inputs are finite; a program needn't handle non-finite values.
Results may differ from a plain program's by a relative error of at most 0.012.
Values may be sent and summed in bfloat16 or wider, within the bound.
A program may use at most 128 MiB of HBM per device.

v0:
```python
import jax
import jax.numpy as jnp
from jax import lax
from jax.sharding import PartitionSpec as P

EXPERTS = 8


epsilon = 1e-05


def from_partner(x, axis, bit):
    return lax.ppermute(x, axis, [(i, i ^ 1 << bit) for i in range(lax.axis_size(axis))])


def choose_rows(expert, routes, gate_share, capacity):
    matches = routes == expert
    member = jnp.any(matches, axis=1)
    slot_rows = jnp.argsort(jnp.where(member, 0, 1).astype(jnp.int32), stable=True)[:capacity]
    filled = jnp.sum(member.astype(jnp.int32))
    occupied = jnp.arange(capacity, dtype=jnp.int32) < filled
    shares = jnp.sum(jnp.where(matches, gate_share, jnp.zeros_like(gate_share)), axis=1)[slot_rows]
    shares = jnp.where(occupied, shares, jnp.zeros_like(shares))
    return (slot_rows, shares, filled)


def local(
    queries,
    cache_keys,
    cache_values,
    new_keys,
    new_values,
    lengths,
    residual,
    out_weight,
    norm_gain,
    router_weight,
    routes,
    gate_tiles,
    up_tiles,
    down_tiles,
):
    factor = queries.shape[-1] ** (-0.5)
    scores = (
        jnp.einsum("rhd,rcd->rhc", queries, cache_keys, preferred_element_type=jnp.float32) * factor
    )
    self_score = (
        jnp.einsum("rhd,rd->rh", queries, new_keys, preferred_element_type=jnp.float32) * factor
    )
    visible = (
        jnp.arange(cache_keys.shape[1], dtype=jnp.int32)[None, None, :] < lengths[:, None, None]
    )
    scores = jnp.where(visible, scores, -1e30)
    highest = jnp.maximum(jnp.max(scores, axis=2), self_score)
    raised = jnp.exp(scores - highest[:, :, None])
    raised_self = jnp.exp(self_score - highest)
    denominator = jnp.sum(raised, axis=2) + raised_self
    weights_cache = (raised / denominator[:, :, None]).astype(jnp.bfloat16)
    weights_self = (raised_self / denominator).astype(jnp.bfloat16)
    context = jnp.einsum(
        "rhc,rcd->rhd", weights_cache, cache_values, preferred_element_type=jnp.float32
    )
    context = (
        context
        + weights_self.astype(jnp.float32)[:, :, None] * new_values.astype(jnp.float32)[:, None, :]
    )
    attended = context.astype(jnp.bfloat16).reshape(queries.shape[0], -1)
    projected = lax.dot_general(
        lax.all_gather(attended, "rank", axis=0, tiled=True),
        out_weight,
        (((1,), (1,)), ((), ())),
        preferred_element_type=jnp.float32,
    )
    hstate = (residual.astype(jnp.float32) + projected).astype(jnp.bfloat16)
    pool_index = lax.axis_index("pool")
    pool_first = pool_index == 0
    other_half = from_partner(hstate, "pool", 0)
    paired = jnp.concatenate(
        [jnp.where(pool_first, hstate, other_half), jnp.where(pool_first, other_half, hstate)],
        axis=0,
    )
    full_rows = lax.all_gather(paired, "rank", axis=1, tiled=True)
    widened = full_rows.astype(jnp.float32)
    mean_square = jnp.mean(widened * widened, axis=1, keepdims=True)
    normed = (widened * lax.rsqrt(mean_square + epsilon) * norm_gain).astype(jnp.bfloat16)
    logits = jnp.dot(normed, router_weight, preferred_element_type=jnp.float32)
    chosen = jax.nn.sigmoid(jnp.take_along_axis(logits, routes, axis=1))
    gate_share = chosen / jnp.sum(chosen, axis=1, keepdims=True)
    total_rows = routes.shape[0]
    block_size = total_rows // EXPERTS
    capacity = 5 * block_size
    rank_count = lax.axis_size("rank")
    tile_count = lax.axis_size("pool") * rank_count // EXPERTS
    device = pool_index * rank_count + lax.axis_index("rank")
    expert = device // tile_count
    slot_rows, shares, filled = choose_rows(expert, routes, gate_share, capacity)
    picked = normed[slot_rows]
    gate_tile = gate_tiles[0]
    up_tile = up_tiles[0]
    down_tile = down_tiles[0]
    gate_part = jnp.dot(picked, gate_tile, preferred_element_type=jnp.float32)
    up_part = jnp.dot(picked, up_tile, preferred_element_type=jnp.float32)
    activated = (jax.nn.silu(gate_part) * up_part).astype(jnp.bfloat16)
    partial_value = jnp.dot(activated, down_tile, preferred_element_type=jnp.float32)
    weighted = partial_value * shares[:, None]
    scattered = jnp.zeros((total_rows, weighted.shape[1]), jnp.float32).at[slot_rows].add(weighted)
    halves = lax.psum_scatter(scattered, "pool", scatter_dimension=0, tiled=True)
    combined = lax.psum_scatter(halves, "rank", scatter_dimension=1, tiled=True)
    return (hstate.astype(jnp.float32) + combined).astype(jnp.bfloat16)


def solution(mesh):
    return jax.shard_map(
        local,
        mesh=mesh,
        in_specs=(
            P(("pool", "rank"), None, None),
            P(("pool", "rank"), None, None),
            P(("pool", "rank"), None, None),
            P(("pool", "rank"), None),
            P(("pool", "rank"), None),
            P(("pool", "rank")),
            P("pool", "rank"),
            P("rank", None),
            P(),
            P(),
            P(),
            P(("pool", "rank"), None, None),
            P(("pool", "rank"), None, None),
            P(("pool", "rank"), None, None),
        ),
        out_specs=P("pool", "rank"),
        check_vma=False,
    )
```

profile of v0, /device:TPU:8, one launch (start us, length us, event | category | flops | bytes accessed | tf_op | source)
XLA Modules:
  0.0 1099.2 jit_solution(6937400700834016821)
XLA Ops:
  8.0 1.8 fusion.47
  9.8 0.9 fusion.48
  11.0 1.6 fusion.22
  13.3 131.1 %all-gather.6.cloned.1.call-done = bf16[128,1,16384]{2,1,0:T(2,128)(2,1)} async-done(((bf16[1,1,16384]{2,1,0:T(2,128)(2,1)}), bf16[128,1,16384]{2,1,0:T(2,128)(2,1)}) %all-gather.6.cloned.1.call-update) | async-done | bytes 4194320 | tf_op jit(solution)/shard_map/all_gather | solution.py:69
  144.4 8.8 fusion.26
  153.2 1.5 collective-permute-start
  154.7 2.3 collective-permute-done
  158.1 113.9 %all-gather.4.cloned.1.call-done = bf16[256,7168]{0,1:T(8,128)(2,1)} async-done(((bf16[256,56]{0,1:T(8,128)(2,1)}), bf16[256,7168]{0,1:T(8,128)(2,1)}) %all-gather.4.cloned.1.call-update) | async-done | bytes 3670032 | tf_op jit(solution)/shard_map/all_gather | solution.py:82
  272.0 3.2 fusion
  275.2 4.5 fusion.2
  279.6 5.9 copy.42
  285.6 2.6 fusion.49
  288.2 4.7 gather_fusion.2
  293.3 0.7 convert_reduce_fusion
  294.0 3.2 sort.17
  297.2 8.0 gather_fusion
  305.2 1.6 gather_fusion.1
  307.5 3.1 fusion.12
  310.6 7.1 convolution_multiply_fusion
  317.7 11.3 %scatter_custom_fusion = f32[256,7168]{1,0:T(8,128)} fusion(s32[160]{0:T(256)S(1)} %compare_select_fusion.1, f32[160,7168]{1,0:T(8,128)} %convolution_multiply_fusion, f32[]{:T(128)} %constant.24.clone.1), kind=kCustom, calls=%fused_computation.13 | custom fusion | flops 1146880 | bytes 7340544 | tf_op jit(solution)/shard_map/scatter-add | solution.py:106
  329.1 90.1 %reduce-scatter.6.cloned.1.call-done = f32[128,7168]{1,0:T(8,128)} async-done(((f32[256,7168]{1,0:T(8,128)}), f32[128,7168]{1,0:T(8,128)}) %reduce-scatter.6.cloned.1.call-update) | async-done | bytes 3670032 | tf_op jit(solution)/shard_map/reduce_scatter | solution.py:107
  419.2 5.3 copy.45
  424.4 666.8 %reduce-scatter.8.cloned.1.call-done = f32[128,56]{0,1:T(8,128)} async-done(((f32[128,7168]{0,1:T(8,128)}), f32[128,56]{0,1:T(8,128)}) %reduce-scatter.8.cloned.1.call-update) | async-done | bytes 28688
  1091.3 1.4 add_convert_fusion
  (40 shorter events, 3.9 us)
Async XLA Ops:
  6.5 304.1 %copy-start = (bf16[1,160,7168]{2,1,0:T(8,128)(2,1)S(1)}, bf16[1,160,7168]{2,1,0:T(8,128)(2,1)}, u32[]{:S(2)}) copy-start(bf16[1,160,7168]{2,1,0:T(8,128)(2,1)} %param.27) | copy-start | bytes 6881284
  6.5 137.9 %copy-start.5 = (bf16[128,56]{0,1:T(8,128)(2,1)S(1)}, bf16[128,56]{0,1:T(8,128)(2,1)}, u32[]{:S(2)}) copy-start(bf16[128,56]{0,1:T(8,128)(2,1)} %param.20) | copy-start | bytes 43012
  6.5 137.9 %all-gather.6.cloned.1.call-start = ((), (), s32[]{:S(2)}) async-start(), calls=%async_computation.4 | async-start | bytes 8454144 | tf_op jit(solution)/shard_map/all_gather | solution.py:69
  12.6 145.1 %copy-start.3 = (s32[256,3]{0,1:T(4,128)S(1)}, s32[256,3]{0,1:T(4,128)}, u32[]{:S(2)}) copy-start(s32[256,3]{0,1:T(4,128)} %param.24) | copy-start | bytes 9220
  13.3 258.7 %all-gather.4.cloned.1.call-start = ((), (), s32[]{:S(2)}) async-start(), calls=%async_computation.2 | async-start | bytes 3698688 | tf_op jit(solution)/shard_map/all_gather | solution.py:82
  153.2 122.0 %copy-start.4 = (f32[7168]{0:T(1024)S(1)}, f32[7168]{0:T(1024)}, u32[]{:S(2)}) copy-start(f32[7168]{0:T(1024)} %param.22) | copy-start | bytes 86020
  153.2 3.8 collective-permute-start
  157.6 261.5 %reduce-scatter.6.cloned.1.call-start = ((), (), s32[]{:S(2)}) async-start(), calls=%async_computation.3 | async-start | bytes 11010048 | tf_op jit(solution)/shard_map/reduce_scatter | solution.py:107
  272.0 3.2 copy-start.1
  279.6 5.9 copy-start.2
  329.0 762.3 %reduce-scatter.8.cloned.1.call-start = ((), (), s32[]{:S(2)}) async-start(), calls=%async_computation.5 | async-start | bytes 3698688
Sparse Core Ops, SparseCore 0:
  13.4 130.9 all-gather.5
  157.8 114.1 all-gather.3
  329.2 89.9 reduce-scatter.5
  424.6 666.6 reduce-scatter.7
where the time goes:
time: 1100 us
  waiting for transfers between devices  1000 us (91%)
  local copies, waits for them, and re-layouts  26.8 us (2%)
  other arithmetic  26.5 us (2%)
  matrix products  25.9 us (2%)
  between operations  14.1 us (1%)
    unnamed x5, waiting for transfers between devices  667 us
    all_gather x1, waiting for transfers between devices, local(): lax.all_gather(attended, 'rank', axis=0, tiled=True)  131 us
    all_gather x1, waiting for transfers between devices, local(): full_rows = lax.all_gather(paired, 'rank', axis=1, tiled=True)  114 us
    reduce_scatter x1, waiting for transfers between devices, local(): lax.psum_scatter(scattered, 'pool', scatter_dimension=0, tiled=True)  90.1 us
  transfers between devices with their start and end apart: 5, of which 5 were waited for; matrix products, arithmetic and copies ran while one was open for 0% of the time, Pallas kernels for 0%

commit v1 on v0

v1 whole, which is shorter than its diff:
```python
import jax
import jax.numpy as jnp
from jax import lax
from jax.experimental import pallas as pl
from jax.experimental.pallas import tpu as pltpu
from jax.sharding import PartitionSpec as P

MESH = pl.DeviceIdType.MESH
BF = jnp.bfloat16
F32 = jnp.float32
EPSILON = 1e-05
SLOTS = 160
WIDE = 112
VM = pl.BlockSpec(memory_space=pltpu.VMEM)
ANY = pl.BlockSpec(memory_space=pl.ANY)


def place(rank):
    return rank // 16, lax.rem(rank // 4, 4), lax.rem(rank // 2, 2), lax.rem(rank, 2)


def rank_of(z, x, yh, c):
    return z * 16 + x * 4 + yh * 2 + c


def iota(shape, dim):
    return lax.broadcasted_iota(jnp.int32, shape, dim)


def dot(a, b):
    return jnp.dot(a, b, preferred_element_type=F32)


def wait_bytes(ref, sem):
    pltpu.make_async_copy(ref, ref, sem).wait()


def gather_kernel(
    att, residual, weight_hbm, h_ref, plane, rows, weight, w_sem, own_sem, p_send, p_recv, up_send,
    up_recv, down_send, down_recv, core_send, core_recv,
):
    pool, rank = lax.axis_index("pool"), lax.axis_index("rank")
    z, x, yh, c = place(rank)
    mine = lax.rem(rank, 16)
    sibling = rank + 1 - 2 * c
    up = rank_of(lax.rem(z + 1, 8), x, yh, c)
    down = rank_of(lax.rem(z + 7, 8), x, yh, c)

    def at(r):
        return (pool, r)

    barrier = pltpu.get_barrier_semaphore()

    def greet(d, _):
        r = z * 16 + lax.rem(mine + d, 16)
        pl.semaphore_signal(barrier, inc=1, device_id=at(r), device_id_type=MESH)
        return 0

    lax.fori_loop(1, 16, greet, 0)
    pl.semaphore_signal(barrier, inc=1, device_id=at(up), device_id_type=MESH)
    pl.semaphore_signal(barrier, inc=1, device_id=at(down), device_id_type=MESH)
    load = pltpu.make_async_copy(weight_hbm, weight, w_sem)
    load.start()
    own = pltpu.make_async_copy(att, plane.at[mine], own_sem)
    own.start()
    pl.semaphore_wait(barrier, 17)

    def to_plane(d, _):
        r = z * 16 + lax.rem(mine + d, 16)
        pltpu.make_async_remote_copy(
            src_ref=att, dst_ref=plane.at[mine], send_sem=p_send, recv_sem=p_recv,
            device_id=at(r), device_id_type=MESH,
        ).start()
        return 0

    lax.fori_loop(1, 16, to_plane, 0)
    own.wait()
    wait_bytes(plane.at[pl.ds(0, 15)], p_recv)

    def turn(k, _):
        part = plane[:, pl.ds(pl.multiple_of(k * 16, 16), 16), :]
        part = jnp.swapaxes(part, 0, 1)
        for s in range(16):
            rows[z, :, pl.ds(pl.multiple_of((k * 16 + s) * 128, 128), 128)] = part[s]
        return 0

    lax.fori_loop(0, 8, turn, 0)

    half = pl.multiple_of(c * 8192, 128)

    def block(b, start, size):
        return rows.at[b, :, pl.ds(pl.multiple_of(half + start, 128), size)]

    def ring(b, start, size, to, send, recv):
        return pltpu.make_async_remote_copy(
            src_ref=block(b, start, size), dst_ref=block(b, start, size), send_sem=send,
            recv_sem=recv, device_id=at(to), device_id_type=MESH,
        )

    def share(b):
        pltpu.make_async_remote_copy(
            src_ref=block(b, 0, 8192), dst_ref=block(b, 0, 8192), send_sem=core_send,
            recv_sem=core_recv, device_id=at(sibling), device_id_type=MESH,
        ).start()

    for s in range(4):
        b_up, b_down = lax.rem(z + 8 - s, 8), lax.rem(z + s, 8)
        size = 8192 if s < 3 else 4096
        a = ring(b_up, 0, size, up, up_send.at[s], up_recv.at[s])
        b = ring(b_down, 8192 - size, size, down, down_send.at[s], down_recv.at[s])
        a.start()
        b.start()
        a.wait()
        b.wait()
        if s < 3:
            share(lax.rem(z + 7 - s, 8))
            share(lax.rem(z + 1 + s, 8))
        else:
            share(lax.rem(z + 4, 8))
    wait_bytes(plane.at[pl.ds(0, 15)], p_send)
    seven = rows.at[pl.ds(0, 7), :, pl.ds(0, 8192)]
    wait_bytes(seven, core_send)
    wait_bytes(seven, core_recv)
    load.wait()
    total = lax.dot_general(
        rows[...].reshape(128, 16384), weight[...], (((1,), (1,)), ((), ())),
        preferred_element_type=F32,
    )
    h_ref[...] = (residual[...].astype(F32) + total).astype(BF)


def expert_kernel(
    h_ref, routes_ref, routes_t_ref, gain_ref, router_ref, gate_hbm, up_hbm, down_hbm, out_ref,
    states, merged, outgoing, slot_in, gathered, normed, gate, up, down_in, down, partial,
    from_core, to_group, from_group, to_rows, from_experts, acc_g, acc_u, acc_r, counts, pick_t,
    w_sem, m_send, m_recv, b_send, b_recv, g_send, g_recv, s_send, s_recv, c_send, c_recv, r_send,
    r_recv, d_send, d_recv,
):
    pool, rank = lax.axis_index("pool"), lax.axis_index("rank")
    z, x, yh, c = place(rank)
    zb = lax.rem(z, 2)
    expert = pool * 4 + z // 2
    spot = zb * 8 + x * 2 + yh
    sibling = rank + 1 - 2 * c

    def member(spot_of, core):
        return (z // 2) * 32 + spot_of * 2 + core

    def pair_of(core, spot_of, i):
        return (4 * (spot_of // 8) + 2 * core + i) * 8 + lax.rem(spot_of, 8)

    def copy(src, dst, send, recv, p, r):
        return pltpu.make_async_remote_copy(
            src_ref=src, dst_ref=dst, send_sem=send, recv_sem=recv, device_id=(p, r),
            device_id_type=MESH,
        )

    zero16 = jnp.zeros((16, SLOTS), BF)

    def load(t, _):
        core, g, i = t // 32, lax.rem(t // 2, 16), lax.rem(t, 2)
        start = pl.multiple_of(pair_of(core, g, i) * WIDE, 16)
        base = pl.multiple_of(t * 128, 128)
        for src, dst in ((gate_hbm, gate), (up_hbm, up)):
            pltpu.make_async_copy(
                src.at[0, pl.ds(start, WIDE), :], dst.at[pl.ds(base, WIDE), :], w_sem.at[0]
            ).start()
        gate[pl.ds(base + WIDE, 16), :] = zero16
        up[pl.ds(base + WIDE, 16), :] = zero16
        return 0

    barrier = pltpu.get_barrier_semaphore()

    def greet(p, r):
        here = jnp.logical_and(p == pool, r == rank)

        @pl.when(jnp.logical_not(here))
        def _():
            pl.semaphore_signal(barrier, inc=1, device_id=(p, r), device_id_type=MESH)

    greet(pool, sibling)
    greet(1 - pool, rank)
    greet(1 - pool, sibling)
    for i in range(2):
        greet(pool, rank_of(4 * zb + 2 * c + i, x, yh, (z // 2) // 2))

    def greet_group(d, _):
        greet(pool, member(lax.rem(spot + d, 16), c))
        return 0

    lax.fori_loop(1, 16, greet_group, 0)

    def greet_sums(e, _):
        greet(e // 4, rank_of(2 * lax.rem(e, 4) + z // 4, x, yh, lax.rem(z // 2, 2)))
        return 0

    lax.fori_loop(0, 8, greet_sums, 0)
    pltpu.make_async_copy(
        down_hbm.at[0], down_in.at[:, pl.ds(0, 7168)], w_sem.at[1]
    ).start()
    lax.fori_loop(0, 64, load, 0)
    down_in[:, pl.ds(7168, 128)] = jnp.zeros((SLOTS, 128), BF)

    shift = (iota((56, 128), 0) + 56 * c == iota((56, 128), 1)).astype(BF)
    states[pool, c] = dot(h_ref[...], shift).astype(BF)

    routes = routes_ref[...]
    lanes8 = iota((256, 8), 1)
    member_t = jnp.zeros((256, 8), F32)
    for k in range(3):
        member_t += (routes[:, k : k + 1] == lanes8).astype(F32)
    member_n = jnp.zeros((8, 256), F32)
    rows8 = iota((8, 256), 0)
    for k in range(3):
        member_n += (routes_t_ref[k : k + 1, :] == rows8).astype(F32)
    r0, r1 = iota((256, 256), 0), iota((256, 256), 1)
    place_n = dot(member_n.astype(BF), (r0 < r1).astype(BF))
    place_t = dot((r1 < r0).astype(BF), member_t.astype(BF))
    counts[...] = jnp.where(member_n > 0.5, place_n, -1.0)
    column = jnp.sum(
        jnp.where(lanes8 == expert, jnp.where(member_t > 0.5, place_t, -1.0), 0.0), axis=1,
        keepdims=True,
    )
    pick_t[...] = (column == iota((256, SLOTS), 1).astype(F32)).astype(BF)

    def pick(e):
        return (counts[pl.ds(e, 1), :] == iota((SLOTS, 256), 0).astype(F32)).astype(BF)

    same = jnp.logical_and(z // 4 == zb, lax.rem(z // 2, 2) == c)
    self_sums = same.astype(jnp.int32)
    self_slots = jnp.logical_and(same, zb == c).astype(jnp.int32)
    pl.semaphore_wait(barrier, 28 - self_sums - self_slots)

    partners = ((pool, sibling), (1 - pool, rank), (1 - pool, sibling))
    sent = []
    for n, (p, r) in enumerate(partners):
        put = copy(states.at[pool, c], states.at[pool, c], m_send.at[n], m_recv.at[n], p, r)
        put.start()
        sent.append(put)
    for put in sent:
        put.wait()
    for p in range(2):
        merged[p * 128 : p * 128 + 128, :] = states[p, 0] + states[p, 1]

    for i in range(2):
        outgoing[i] = dot(pick(pool * 4 + 2 * c + i), merged[...]).astype(BF)
    for i in range(2):
        r = rank_of(2 * (2 * c + i) + z // 4, x, yh, lax.rem(z // 2, 2))
        src, dst = outgoing.at[i], slot_in.at[lax.rem(z, 2)]

        @pl.when(r == rank)
        def _():
            pltpu.make_async_copy(src, dst, b_recv.at[lax.rem(z, 2)]).start()

        @pl.when(r != rank)
        def _():
            copy(src, dst, b_send.at[i], b_recv.at[lax.rem(z, 2)], pool, r).start()

    for i in range(2):
        wait_bytes(slot_in.at[i], b_recv.at[i])

    mine = gathered.at[c, spot]
    own = pltpu.make_async_copy(slot_in, mine, w_sem.at[2])
    own.start()

    def to_group_start(d, _):
        to = lax.rem(spot + d, 16)
        copy(slot_in, mine, g_send, g_recv.at[spot], pool, member(to, c)).start()
        return 0

    lax.fori_loop(1, 16, to_group_start, 0)
    own.wait()
    copy(slot_in, mine, s_send, s_recv, pool, sibling).start()

    def pass_on(d, _):
        frm = lax.rem(spot + d, 16)
        wait_bytes(gathered.at[c, frm], g_recv.at[frm])
        copy(
            gathered.at[c, frm], gathered.at[c, frm], s_send, s_recv, pool, sibling
        ).start()
        return 0

    lax.fori_loop(1, 16, pass_on, 0)

    wait_bytes(down_hbm.at[0], w_sem.at[1])

    def cut(t, _):
        core, g, i = t // 32, lax.rem(t // 2, 16), lax.rem(t, 2)
        start = pair_of(core, g, i) * WIDE
        window = down_in[:, pl.ds(pl.multiple_of(start // 128 * 128, 128), 256)]
        a, b = iota((256, 128), 0), iota((256, 128), 1)
        shift = jnp.logical_and(a == b + lax.rem(start, 128), b < WIDE).astype(BF)
        down[t] = dot(window, shift).astype(BF)
        return 0

    lax.fori_loop(0, 64, cut, 0)
    wait_bytes(gathered.at[0], s_recv)

    def squares(t, total):
        v = gathered[t // 32, lax.rem(t // 2, 16), lax.rem(t, 2)].astype(F32)
        return total + v * v

    total = lax.fori_loop(0, 64, squares, jnp.zeros((SLOTS, 128), F32))
    inv = lax.rsqrt(jnp.sum(total, axis=1, keepdims=True) * (1.0 / 7168) + EPSILON)

    def norm(t, _):
        core, g, i = t // 32, lax.rem(t // 2, 16), lax.rem(t, 2)
        v = gathered[core, g, i].astype(F32)
        scaled = v * inv * gain_ref[pl.ds(pair_of(core, g, i), 1), :]
        normed[:, pl.ds(pl.multiple_of(t * 128, 128), 128)] = scaled.astype(BF)
        return 0

    lax.fori_loop(0, 64, norm, 0)

    acc_g[...] = jnp.zeros_like(acc_g)
    acc_u[...] = jnp.zeros_like(acc_u)
    acc_r[...] = jnp.zeros_like(acc_r)
    all_w = gate_hbm.at[0]
    wait_bytes(all_w, w_sem.at[0])
    wait_bytes(all_w, w_sem.at[0])

    def multiply(u, _):
        k = pl.ds(pl.multiple_of(u * 1024, 1024), 1024)
        left = normed[:, k]
        acc_g[...] += dot(left, gate[k, :])
        acc_u[...] += dot(left, up[k, :])
        acc_r[...] += dot(left, router_ref[k, :])
        return 0

    lax.fori_loop(0, 8, multiply, 0)
    chosen = jax.nn.sigmoid(acc_r[...])
    named = dot(pick(expert), member_t.astype(BF))
    whole = jnp.sum(chosen * named, axis=1, keepdims=True)
    own_share = jnp.sum(jnp.where(iota((SLOTS, 8), 1) == expert, chosen * named, 0.0), axis=1, keepdims=True)
    filled = jnp.sum(named, axis=1, keepdims=True) > 0.5
    share = jnp.where(filled, own_share / jnp.where(filled, whole, 1.0), 0.0)
    hidden = (jax.nn.silu(acc_g[...]) * acc_u[...]).astype(BF)

    def product(core, n):
        t = core * 32 + n
        partial[core, n // 2, lax.rem(n, 2)] = (dot(hidden, down[t]) * share).astype(BF)

    def other_half(n, _):
        product(1 - c, n)
        return 0

    lax.fori_loop(0, 32, other_half, 0)
    swap = copy(partial.at[1 - c], from_core, c_send, c_recv, pool, sibling)
    swap.start()

    def own_half(n, _):
        product(c, n)
        return 0

    lax.fori_loop(0, 32, own_half, 0)
    swap.wait()

    def chip_sum(d, _):
        to = lax.rem(spot + d, 16)
        to_group[to] = (partial[c, to].astype(F32) + from_core[to].astype(F32)).astype(BF)
        copy(
            to_group.at[to], from_group.at[spot], r_send, r_recv, pool, member(to, c)
        ).start()
        return 0

    lax.fori_loop(1, 16, chip_sum, 0)
    from_group[spot] = (partial[c, spot].astype(F32) + from_core[spot].astype(F32)).astype(BF)
    wait_bytes(from_group.at[pl.ds(0, 15)], r_recv)

    for i in range(2):
        def add(s, total):
            return total + from_group[s, i].astype(F32)

        total = lax.fori_loop(0, 16, add, jnp.zeros((SLOTS, 128), F32))
        spread = dot(pick_t[...], total.astype(BF)).astype(BF)
        for p in range(2):
            to_rows[i, p] = spread[p * 128 : p * 128 + 128, :]
        for p in range(2):
            for core in range(2):
                r = rank_of(4 * zb + 2 * c + i, x, yh, core)
                src, dst = to_rows.at[i, p], from_experts.at[expert]
                here = jnp.logical_and(pool == p, r == rank)

                @pl.when(here)
                def _():
                    pltpu.make_async_copy(src, dst, d_recv).start()

                @pl.when(jnp.logical_not(here))
                def _():
                    copy(src, dst, d_send, d_recv, p, r).start()

    wait_bytes(from_experts, d_recv)
    sums = jnp.zeros((128, 128), F32)
    for e in range(8):
        sums += from_experts[e].astype(F32)
    back = (iota((128, 56), 0) == iota((128, 56), 1) + 56 * c).astype(F32)
    mine_sum = jnp.dot(sums, back, preferred_element_type=F32, precision=lax.Precision.HIGHEST)
    out_ref[...] = (h_ref[...].astype(F32) + mine_sum).astype(BF)

    for i in range(2):
        r = rank_of(2 * (2 * c + i) + z // 4, x, yh, lax.rem(z // 2, 2))

        @pl.when(r != rank)
        def _():
            wait_bytes(outgoing.at[i], b_send.at[i])

    wait_bytes(gathered.at[0, pl.ds(0, 15)], g_send)
    wait_bytes(gathered.at[0], s_send)
    wait_bytes(from_group.at[pl.ds(0, 15)], r_send)
    wait_bytes(from_experts.at[pl.ds(0, 7)], d_send)

    @pl.when(jnp.logical_not(same))
    def _():
        wait_bytes(from_experts.at[0], d_send)


def attention(queries, cache_keys, cache_values, new_keys, new_values, lengths):
    factor = queries.shape[-1] ** (-0.5)
    scores = jnp.einsum("rhd,rcd->rhc", queries, cache_keys, preferred_element_type=F32) * factor
    self_score = jnp.einsum("rhd,rd->rh", queries, new_keys, preferred_element_type=F32) * factor
    visible = jnp.arange(cache_keys.shape[1], dtype=jnp.int32)[None, None, :] < lengths[:, None, None]
    scores = jnp.where(visible, scores, -1e30)
    highest = jnp.maximum(jnp.max(scores, axis=2), self_score)
    raised = jnp.exp(scores - highest[:, :, None])
    raised_self = jnp.exp(self_score - highest)
    denominator = jnp.sum(raised, axis=2) + raised_self
    weights_cache = (raised / denominator[:, :, None]).astype(BF)
    weights_self = (raised_self / denominator).astype(BF)
    context = jnp.einsum("rhc,rcd->rhd", weights_cache, cache_values, preferred_element_type=F32)
    context = context + weights_self.astype(F32)[:, :, None] * new_values.astype(F32)[:, None, :]
    return context.astype(BF)


def local(
    queries, cache_keys, cache_values, new_keys, new_values, lengths, residual, out_weight,
    norm_gain, router_weight, routes, gate_tiles, up_tiles, down_tiles,
):
    attended = attention(queries, cache_keys, cache_values, new_keys, new_values, lengths)
    dma = pltpu.SemaphoreType.DMA
    hstate = pl.pallas_call(
        gather_kernel,
        out_shape=jax.ShapeDtypeStruct((128, 56), BF),
        in_specs=[VM, VM, ANY],
        out_specs=VM,
        scratch_shapes=[
            pltpu.VMEM((16, 128, 128), BF),
            pltpu.VMEM((8, 16, 16384), BF),
            pltpu.VMEM((56, 16384), BF),
            dma, dma, dma, dma, dma((4,)), dma((4,)), dma((4,)), dma((4,)), dma, dma,
        ],
        compiler_params=pltpu.CompilerParams(
            collective_id=0, has_side_effects=True, vmem_limit_bytes=48 * 2**20
        ),
        name="gather_project",
    )(attended.reshape(128, 128), residual, out_weight)
    gain = jnp.pad(norm_gain.reshape(64, WIDE), ((0, 0), (0, 16)))
    router = jnp.pad(router_weight.reshape(64, WIDE, 8), ((0, 0), (0, 16), (0, 0)))
    router = router.reshape(2, 2, 2, 8, 128, 8).transpose(1, 0, 3, 2, 4, 5).reshape(8192, 8)
    return pl.pallas_call(
        expert_kernel,
        out_shape=jax.ShapeDtypeStruct((128, 56), BF),
        in_specs=[VM, VM, VM, VM, VM, ANY, ANY, ANY],
        out_specs=VM,
        scratch_shapes=[
            pltpu.VMEM((2, 2, 128, 128), BF),
            pltpu.VMEM((256, 128), BF),
            pltpu.VMEM((2, SLOTS, 128), BF),
            pltpu.VMEM((2, SLOTS, 128), BF),
            pltpu.VMEM((2, 16, 2, SLOTS, 128), BF),
            pltpu.VMEM((SLOTS, 8192), BF),
            pltpu.VMEM((8192, SLOTS), BF),
            pltpu.VMEM((8192, SLOTS), BF),
            pltpu.VMEM((SLOTS, 7296), BF),
            pltpu.VMEM((64, SLOTS, 128), BF),
            pltpu.VMEM((2, 16, 2, SLOTS, 128), BF),
            pltpu.VMEM((16, 2, SLOTS, 128), BF),
            pltpu.VMEM((16, 2, SLOTS, 128), BF),
            pltpu.VMEM((16, 2, SLOTS, 128), BF),
            pltpu.VMEM((2, 2, 128, 128), BF),
            pltpu.VMEM((8, 128, 128), BF),
            pltpu.VMEM((SLOTS, SLOTS), F32),
            pltpu.VMEM((SLOTS, SLOTS), F32),
            pltpu.VMEM((SLOTS, 8), F32),
            pltpu.VMEM((8, 256), F32),
            pltpu.VMEM((256, SLOTS), BF),
            dma((3,)), dma((3,)), dma((3,)), dma((2,)), dma((2,)), dma, dma((16,)), dma, dma, dma,
            dma, dma, dma, dma, dma,
        ],
        compiler_params=pltpu.CompilerParams(
            collective_id=1, has_side_effects=True, vmem_limit_bytes=56 * 2**20
        ),
        name="experts",
    )(hstate, routes, routes.T, gain, router, gate_tiles, up_tiles, down_tiles)


def solution(mesh):
    return jax.shard_map(
        local,
        mesh=mesh,
        in_specs=(
            P(("pool", "rank"), None, None),
            P(("pool", "rank"), None, None),
            P(("pool", "rank"), None, None),
            P(("pool", "rank"), None),
            P(("pool", "rank"), None),
            P(("pool", "rank")),
            P("pool", "rank"),
            P("rank", None),
            P(),
            P(),
            P(),
            P(("pool", "rank"), None, None),
            P(("pool", "rank"), None, None),
            P(("pool", "rank"), None, None),
        ),
        out_specs=P("pool", "rank"),
        check_vma=False,
    )
```

time: 1100 us -> 165 us (0.15)
  the two profiles are of different devices: /device:TPU:8 before, /device:TPU:55 now
where the time goes in v1:
time: 165 us; the launch traced here: 164 us
  Pallas kernels  143 us (87%)
  local copies, waits for them, and re-layouts  16.5 us (10%)
  matrix products  3.14 us (2%)
    pallas_call x1, Pallas kernels, local(): pl.pallas_call(expert_kernel, out_shape=jax.ShapeDtypeStruct((128, 56), B...  96 us
    pallas_call x1, Pallas kernels, local(): pl.pallas_call(gather_kernel, out_shape=jax.ShapeDtypeStruct((128, 56), B...  46.6 us
    unnamed x16, local copies, waits for them, and re-layouts  10.7 us

profile of v1, /device:TPU:55, one launch (start us, length us, event | category | flops | bytes accessed | tf_op | source)
XLA Modules:
  0.0 164.0 jit_solution(6678607994318982305)
XLA Ops:
  0.0 0.0 copy-start
  0.7 0.7 mul.41
  1.4 0.8 copy.26.residual
  2.3 0.8 reshape.88
  3.1 0.6 pad.8.gain_ref
  3.7 1.1 reshape.89
  4.8 1.5 copy.29.routes_ref
  6.3 0.0 copy-done
  6.3 1.4 fusion.12
  7.8 0.0 copy-done.4
  7.8 0.0 copy-done.5
  7.8 0.1 fusion.13
  7.9 0.3 fusion.5
  8.2 1.6 fusion.1
  9.8 0.0 copy-done.1
  9.8 46.6 %gather_project.1.h_ref = bf16[128,56]{1,0:T(8,128)(2,1)S(1)} custom-call(bf16[128,128]{1,0:T(8,128)(2,1)S(1)} %reshape.87.att, bf16[128,56]{1,0:T(8,128)(2,1)S(1)} %copy.26.residual, bf16[56,16384]{1,0:T(8,128)(2,1)S(1)} %copy-done.1), custom_call_target="tpu_custom_call" | custom-call | tf_op jit(solution)/shard_map/gather_project/pallas_call | solution.py:440
  56.4 0.0 copy-start.2
  56.4 0.6 copy-done.2
  57.0 1.8 %copy.28 = bf16[2,2,8,2,128,8]{5,4,3,2,1,0:T(8,128)(2,1)} copy(bf16[2,2,8,2,128,8]{4,2,3,0,1,5:T(8,128)(2,1)S(1)} %bitcast.37) | data formatting | bytes 262144 | tf_op jit(solution)/shard_map/transpose | solution.py:458
  58.8 4.8 %copy.30.gate_hbm = bf16[1,7168,160]{2,1,0:T(8,128)(2,1)} copy(bf16[1,7168,160]{1,2,0:T(8,128)(2,1)} %param.25) | data formatting | bytes 4587520 | tf_op args[11]
  63.6 0.0 copy-done.3
  63.6 3.0 %copy.31.up_hbm = bf16[1,7168,160]{2,1,0:T(8,128)(2,1)} copy(bf16[1,7168,160]{1,2,0:T(8,128)(2,1)S(1)} %copy-done.3) | data formatting | bytes 4587520 | tf_op args[12]
  66.6 96.0 %experts.1 = bf16[128,56]{1,0:T(8,128)(2,1)} custom-call(bf16[128,56]{1,0:T(8,128)(2,1)} %copy-done.2, s32[256,3]{1,0:T(8,128)} %copy.29.routes_ref, s32[3,256]{1,0:T(4,128)} %bitcast.38, f32[64,128]{1,0:T(8,128)} %pad.8.gain_ref, bf16[8192,8]{1,0:T(8,128)(2,1)} %bitcast.36, bf16[1,7168,160]{2,1,0:T(8,128)(2,1)} %copy.30.gate_hbm, ...), custom_call_target="tpu_custom_call" | custom-call | tf_op jit(solution)/shard_map/experts/pallas_call | solution.py:459
  162.6 1.4 copy.32
  (8 shorter events, 0.1 us)
Async XLA Ops:
  0.0 6.3 %copy-start = (bf16[1,2048,256]{2,1,0:T(8,128)(2,1)S(1)}, bf16[1,2048,256]{2,1,0:T(8,128)(2,1)}, u32[]{:S(2)}) copy-start(bf16[1,2048,256]{2,1,0:T(8,128)(2,1)} %param.15) | copy-start | bytes 3145732
  0.0 7.8 %copy-start.4 = (bf16[1,64,256]{2,1,0:T(8,128)(2,1)S(1)}, bf16[1,64,256]{2,1,0:T(8,128)(2,1)}, u32[]{:S(2)}) copy-start(bf16[1,64,256]{2,1,0:T(8,128)(2,1)} %param.14) | copy-start | bytes 98308
  0.0 7.8 %copy-start.5 = (bf16[1,256]{1,0:T(2,128)(2,1)S(1)}, bf16[1,256]{1,0:T(2,128)(2,1)}, u32[]{:S(2)}) copy-start(bf16[1,256]{1,0:T(2,128)(2,1)} %param.17) | copy-start | bytes 1540
  6.3 3.5 %copy-start.1 = (bf16[56,16384]{1,0:T(8,128)(2,1)S(1)}, bf16[56,16384]{1,0:T(8,128)(2,1)}, u32[]{:S(2)}) copy-start(bf16[56,16384]{1,0:T(8,128)(2,1)} %weight_hbm.1) | copy-start | bytes 5505028
  56.4 0.6 copy-start.2
  58.8 4.8 %copy-start.3 = (bf16[1,7168,160]{1,2,0:T(8,128)(2,1)S(1)}, bf16[1,7168,160]{1,2,0:T(8,128)(2,1)}, u32[]{:S(2)}) copy-start(bf16[1,7168,160]{1,2,0:T(8,128)(2,1)} %param.26) | copy-start | bytes 6881284

commit v2 on v0

v2 whole, which is shorter than its diff:
```python
import jax
import jax.numpy as jnp
from jax import lax
from jax.experimental import pallas as pl
from jax.experimental.pallas import tpu as pltpu
from jax.sharding import PartitionSpec as P

MESH = pl.DeviceIdType.MESH
BF = jnp.bfloat16
F32 = jnp.float32
EPSILON = 1e-05
SLOTS = 160
WIDE = 112
VM = pl.BlockSpec(memory_space=pltpu.VMEM)
ANY = pl.BlockSpec(memory_space=pl.ANY)


def place(rank):
    return rank // 16, lax.rem(rank // 4, 4), lax.rem(rank // 2, 2), lax.rem(rank, 2)


def rank_of(z, x, yh, c):
    return z * 16 + x * 4 + yh * 2 + c


def iota(shape, dim):
    return lax.broadcasted_iota(jnp.int32, shape, dim)


def dot(a, b):
    return jnp.dot(a, b, preferred_element_type=F32)


def wait_bytes(ref, sem):
    pltpu.make_async_copy(ref, ref, sem).wait()


def padded(tiles):
    out = []
    for j in range(8):
        parts = []
        if j > 0:
            parts.append(tiles[j - 1][:, 128 - 16 * j :])
        if j < 7:
            parts.append(tiles[j][:, : WIDE - 16 * j])
        parts.append(jnp.zeros((tiles[0].shape[0], 16), tiles[0].dtype))
        out.append(jnp.concatenate([part for part in parts if part.shape[1]], axis=1))
    return out


def lane_tile(n):
    return pl.ds(pl.multiple_of(n * 128, 128), 128)


def layer_kernel(
    queries_hbm, keys_hbm, values_hbm, new_key_ref, new_value_ref, length_ref, residual_hbm,
    weight_hbm, gain_ref, router_ref, routes_ref, gate_hbm, up_hbm, down_hbm, out_ref,
    queries, keys, values, residual, weight, gate, up, down, fused, cut, rows_in, rows, states_in,
    state_sent, states, acc, partial, from_core, to_group, from_group, to_rows, from_experts,
    places, load_sem, a_plane, a_plane_in, a_ring, a_up_in, a_down_in, a_core, a_core_in, b_plane,
    b_plane_in, b_ring, b_up_in, b_down_in, b_core, b_core_in, m_send, m_recv, c_send, c_recv,
    r_send, r_recv, d_send, d_recv,
):
    pool, rank = lax.axis_index("pool"), lax.axis_index("rank")
    z, x, yh, c = place(rank)
    zb = lax.rem(z, 2)
    expert = pool * 4 + z // 2
    spot = zb * 8 + x * 2 + yh
    sibling = rank + 1 - 2 * c
    up_rank = rank_of(lax.rem(z + 1, 8), x, yh, c)
    down_rank = rank_of(lax.rem(z + 7, 8), x, yh, c)
    across = (pool == c).astype(jnp.int32)
    same = jnp.logical_and(z // 4 == zb, lax.rem(z // 2, 2) == c)

    def member(spot_of, core):
        return (z // 2) * 32 + spot_of * 2 + core

    def copy(src, dst, send, recv, p, r):
        return pltpu.make_async_remote_copy(
            src_ref=src, dst_ref=dst, send_sem=send, recv_sem=recv, device_id=(p, r),
            device_id_type=MESH,
        )

    def is_self(p, r):
        return jnp.logical_and(p == pool, r == rank)

    loads = []
    for n, (src, dst) in enumerate((
        (queries_hbm.at[0], queries), (keys_hbm.at[0], keys), (values_hbm.at[0], values),
        (residual_hbm, residual), (weight_hbm, weight), (gate_hbm.at[0], gate),
        (up_hbm.at[0], up), (down_hbm.at[0], down),
    )):
        load = pltpu.make_async_copy(src, dst, load_sem.at[n])
        load.start()
        loads.append(load)

    barrier = pltpu.get_barrier_semaphore()

    def greet(p, r):
        @pl.when(jnp.logical_not(is_self(p, r)))
        def _():
            pl.semaphore_signal(barrier, inc=1, device_id=(p, r), device_id_type=MESH)

    def greet_plane(d, _):
        greet(pool, z * 16 + lax.rem(x * 2 + yh + d, 8) * 2 + c)
        return 0

    def greet_group(d, _):
        greet(pool, member(lax.rem(spot + d, 16), c))
        return 0

    def greet_sums(e, _):
        greet(e // 4, rank_of(2 * lax.rem(e, 4) + z // 4, x, yh, lax.rem(z // 2, 2)))
        return 0

    lax.fori_loop(1, 8, greet_plane, 0)
    greet(pool, sibling)
    greet(pool, up_rank)
    greet(pool, down_rank)
    for core in range(2):
        greet(c, rank - c + core)
    lax.fori_loop(1, 16, greet_group, 0)
    lax.fori_loop(0, 8, greet_sums, 0)

    loads[0].wait()
    loads[1].wait()
    q = queries[...]
    scores = lax.dot_general(
        q, keys[...], (((1,), (1,)), ((), ())), preferred_element_type=F32
    ) * (1.0 / 16.0)
    self_score = jnp.sum(
        q.astype(F32) * new_key_ref[...].astype(F32), axis=1, keepdims=True
    ) * (1.0 / 16.0)
    scores = jnp.where(iota((64, 2048), 1) < length_ref[0], scores, -1e30)
    highest = jnp.maximum(jnp.max(scores, axis=1, keepdims=True), self_score)
    raised = jnp.exp(scores - highest)
    raised_self = jnp.exp(self_score - highest)
    denominator = jnp.sum(raised, axis=1, keepdims=True) + raised_self
    weights = (raised / denominator).astype(BF)
    weight_self = (raised_self / denominator).astype(BF).astype(F32)
    loads[2].wait()
    context = dot(weights, values[...]) + weight_self * new_value_ref[...].astype(F32)
    context = context.astype(BF)
    rows_in[z, x, yh, c, 0:64, :] = context[:, 0:128]
    rows_in[z, x, yh, c, 64:128, :] = context[:, 128:256]

    pl.semaphore_wait(barrier, 35 - across - same.astype(jnp.int32))

    def gather(buf, plane, plane_in, ring, up_in, down_in, core_send, core_in, work):
        own = buf.at[z, x, yh, c]
        flat = x * 2 + yh

        def to_plane(d, _):
            r = z * 16 + lax.rem(flat + d, 8) * 2 + c
            copy(own, own, plane, plane_in.at[flat], pool, r).start()
            return 0

        lax.fori_loop(1, 8, to_plane, 0)
        work(-1)

        def landed(d, _):
            j = lax.rem(flat + d, 8)
            wait_bytes(buf.at[z, j // 2, lax.rem(j, 2), c], plane_in.at[j])
            return 0

        lax.fori_loop(1, 8, landed, 0)

        def chunk(b, k):
            return buf.at[b, pl.ds(2 * k, 2), :, c]

        def share(b, k):
            copy(chunk(b, k), chunk(b, k), core_send, core_in.at[b], pool, sibling).start()

        for s in range(5):
            b_up, b_down = lax.rem(z + 8 - s, 8), lax.rem(z + s, 8)
            for k in range(2):
                if s > 0 and (s < 4 or k == 0):
                    wait_bytes(chunk(b_up, k), up_in.at[s - 1, k])
                if s < 3 or (s == 3 and k == 0):
                    copy(chunk(b_up, k), chunk(b_up, k), ring.at[0], up_in.at[s, k], pool, up_rank).start()
                if s > 0 and (s < 4 or k == 1):
                    wait_bytes(chunk(b_down, k), down_in.at[s - 1, k])
                if s < 3 or (s == 3 and k == 1):
                    copy(chunk(b_down, k), chunk(b_down, k), ring.at[1], down_in.at[s, k], pool, down_rank).start()
                if s < 4 or k == 0:
                    share(b_up, k)
                if 0 < s < 4 or (s == 4 and k == 1):
                    share(b_down, k)
            work(s)
        seven = buf.at[pl.ds(0, 7), pl.ds(0, 2), :, c]
        wait_bytes(buf.at[pl.ds(0, 7), 0, 0, c], plane)
        wait_bytes(seven, ring.at[0])
        wait_bytes(seven, ring.at[1])
        wait_bytes(buf.at[:, :, :, c], core_send)

    def from_sibling(buf, core_in, b):
        wait_bytes(buf.at[b, :, :, c], core_in.at[b])

    def step_planes(s):
        if s in (0, 4):
            return [lax.rem(z + s, 8)]
        return [lax.rem(z + 8 - s, 8), lax.rem(z + s, 8)]

    def prepare(b, _):
        gains = padded([gain_ref[:, lane_tile(b * 7 + j)] for j in range(7)])
        routers = padded([router_ref[:, lane_tile(b * 7 + j)].astype(F32) for j in range(7)])
        for j in range(8):
            part = (routers[j] * gains[j]).astype(BF)
            fused[320:336, lane_tile(b * 8 + j)] = jnp.concatenate([part, jnp.zeros_like(part)], axis=0)

        def strip(n, _):
            r = pl.ds(pl.multiple_of(n * 32, 32), 32)
            for src, first in ((gate, 0), (up, SLOTS)):
                tiles = padded([src[r, lane_tile(b * 7 + j)] for j in range(7)])
                to = pl.ds(pl.multiple_of(first + n * 32, 32), 32)
                for j in range(8):
                    fused[to, lane_tile(b * 8 + j)] = (tiles[j].astype(F32) * gains[j]).astype(BF)
            tiles = padded([down[r, lane_tile(b * 7 + j)] for j in range(7)])
            for j in range(8):
                cut[r, lane_tile(b * 8 + j)] = tiles[j]
            return 0

        lax.fori_loop(0, 5, strip, 0)
        return 0

    def turn(b):
        def part(k, _):
            block = rows_in[b, :, :, :, pl.ds(pl.multiple_of(k * 16, 16), 16), :]
            block = jnp.swapaxes(block.reshape(16, 16, 128), 0, 1)
            for j in range(16):
                n = 2 * (lax.rem(k, 4) * 16 + j) + k // 4
                rows[b, :, lane_tile(n)] = block[j]
            return 0

        lax.fori_loop(0, 8, part, 0)

    def row_work(s):
        if s < 0:
            return
        if s == 0:
            for load in loads[5:]:
                load.wait()
        if s < 4:
            lax.fori_loop(2 * s, 2 * s + 2, prepare, 0)
        for b in step_planes(s):
            from_sibling(rows_in, a_core_in, b)
            turn(b)

    gather(rows_in, a_plane, a_plane_in, a_ring, a_up_in, a_down_in, a_core, a_core_in, row_work)

    loads[3].wait()
    loads[4].wait()
    projected = lax.dot_general(
        rows[...].reshape(128, 16384), weight[...], (((1,), (1,)), ((), ())),
        preferred_element_type=F32,
    )
    hstate = (residual[...].astype(F32) + projected).astype(BF)

    shift = (iota((56, 128), 0) + 56 * c == iota((56, 128), 1)).astype(BF)
    state_sent[...] = dot(hstate, shift).astype(BF)
    for p in range(2):
        r = rank - c + pool
        here = is_self(p, r)

        @pl.when(here)
        def _():
            pltpu.make_async_copy(state_sent, states_in.at[c], m_recv.at[c]).start()

        @pl.when(jnp.logical_not(here))
        def _():
            copy(state_sent, states_in.at[c], m_send, m_recv.at[c], p, r).start()

    rows8 = iota((8, 256), 0)
    members = jnp.zeros((8, 256), F32)
    for k in range(3):
        members += (routes_ref[k : k + 1, :] == rows8).astype(F32)
    r0, r1 = iota((256, 256), 0), iota((256, 256), 1)
    order = dot(members.astype(BF), (r0 < r1).astype(BF))
    places[...] = jnp.where(members > 0.5, order, -1.0)
    own_places = places[pl.ds(expert, 1), :]
    picked = own_places == iota((SLOTS, 256), 0).astype(F32)
    pick = picked.astype(BF)
    acc[...] = jnp.zeros_like(acc)
    for i in range(2):
        wait_bytes(state_sent, m_recv.at[i])
    states[z, x, yh, c] = states_in[0] + states_in[1]

    def state_work(s):
        if s < 0:
            return
        for b in step_planes(s):
            from_sibling(states, b_core_in, b)
            halves = []
            for core in range(2):
                halves.append(jnp.concatenate(
                    [states[b, i // 2, i % 2, core] for i in range(8)], axis=1
                ))
            plane = jnp.concatenate(halves, axis=0)
            wide = plane.astype(F32)
            k = pl.ds(pl.multiple_of(b * 1024, 1024), 1024)
            product = lax.dot_general(
                fused[:, k], plane, (((1,), (1,)), ((), ())), preferred_element_type=F32
            )
            acc[0:336, :] += product
            square = wide * wide
            lanes = square[:, 0:128]
            for i in range(1, 8):
                lanes += square[:, i * 128 : i * 128 + 128]
            acc[336:344, :] += lax.dot_general(
                jnp.ones((8, 128), F32), lanes, (((1,), (1,)), ((), ())),
                preferred_element_type=F32, precision=lax.Precision.HIGHEST,
            )

    gather(states, b_plane, b_plane_in, b_ring, b_up_in, b_down_in, b_core, b_core_in, state_work)

    inv = lax.rsqrt(acc[336:337, :] * (1.0 / 7168) + EPSILON)
    chosen = jax.nn.sigmoid(acc[320:328, :] * inv)
    named = jnp.where(members > 0.5, chosen, 0.0)
    whole = jnp.sum(named, axis=0, keepdims=True)
    row_share = jnp.sum(jnp.where(rows8 == expert, named, 0.0), axis=0, keepdims=True) / whole
    hidden_t = (jax.nn.silu(acc[0:160, :] * inv) * (acc[160:320, :] * inv)).astype(BF)
    hidden = lax.dot_general(
        pick, hidden_t, (((1,), (1,)), ((), ())), preferred_element_type=F32
    ).astype(BF)
    share = jnp.sum(jnp.where(picked, row_share, 0.0), axis=1, keepdims=True)

    def product(core, n):
        b = 4 * (n // 2) + 2 * core + lax.rem(n, 2)
        k = pl.ds(pl.multiple_of(b * 1024, 1024), 1024)
        sums = (dot(hidden, cut[:, k]) * share).astype(BF)
        for j in range(8):
            partial[core, n // 2, j, lax.rem(n, 2)] = sums[:, j * 128 : j * 128 + 128]

    def other_half(n, _):
        product(1 - c, n)
        copy(
            partial.at[1 - c, n // 2, :, lax.rem(n, 2)], from_core.at[n // 2, :, lax.rem(n, 2)],
            c_send, c_recv, pool, sibling,
        ).start()
        return 0

    def own_half(n, _):
        product(c, n)
        return 0

    lax.fori_loop(0, 4, other_half, 0)
    lax.fori_loop(0, 4, own_half, 0)
    wait_bytes(from_core, c_recv)

    def chip_sum(spot_of):
        g, j = spot_of // 8, lax.rem(spot_of, 8)
        return (partial[c, g, j].astype(F32) + from_core[g, j].astype(F32)).astype(BF)

    def send_sum(d, _):
        to = lax.rem(spot + d, 16)
        to_group[to] = chip_sum(to)
        copy(
            to_group.at[to], from_group.at[spot], r_send, r_recv, pool, member(to, c)
        ).start()
        return 0

    lax.fori_loop(1, 16, send_sum, 0)
    from_group[spot] = chip_sum(spot)

    column = lax.dot_general(
        (r0 == r1).astype(BF), jnp.broadcast_to(own_places, (8, 256)).astype(BF),
        (((1,), (1,)), ((), ())), preferred_element_type=F32,
    )[:, 0:1]
    spread_by = (column == iota((256, SLOTS), 1).astype(F32)).astype(BF)
    wait_bytes(from_group.at[pl.ds(0, 15)], r_recv)

    for i in range(2):
        total = from_group[0, i].astype(F32)
        for s in range(1, 16):
            total += from_group[s, i].astype(F32)
        spread = dot(spread_by, total.astype(BF)).astype(BF)
        for p in range(2):
            to_rows[i, p] = spread[p * 128 : p * 128 + 128, :]
        for p in range(2):
            for core in range(2):
                r = rank_of(4 * zb + 2 * c + i, x, yh, core)
                src, dst = to_rows.at[i, p], from_experts.at[expert]
                here = is_self(p, r)

                @pl.when(here)
                def _():
                    pltpu.make_async_copy(src, dst, d_recv).start()

                @pl.when(jnp.logical_not(here))
                def _():
                    copy(src, dst, d_send, d_recv, p, r).start()

    wait_bytes(from_experts, d_recv)
    sums = from_experts[0].astype(F32)
    for e in range(1, 8):
        sums += from_experts[e].astype(F32)
    back = (iota((128, 56), 0) == iota((128, 56), 1) + 56 * c).astype(F32)
    mine_sum = jnp.dot(sums, back, preferred_element_type=F32, precision=lax.Precision.HIGHEST)
    out_ref[...] = (hstate.astype(F32) + mine_sum).astype(BF)

    wait_bytes(state_sent, m_send)

    @pl.when(across == 0)
    def _():
        wait_bytes(state_sent, m_send)

    wait_bytes(from_core, c_send)
    wait_bytes(from_group.at[pl.ds(0, 15)], r_send)
    wait_bytes(from_experts.at[pl.ds(0, 7)], d_send)

    @pl.when(jnp.logical_not(same))
    def _():
        wait_bytes(from_experts.at[0], d_send)


def local(
    queries, cache_keys, cache_values, new_keys, new_values, lengths, residual, out_weight,
    norm_gain, router_weight, routes, gate_tiles, up_tiles, down_tiles,
):
    dma = pltpu.SemaphoreType.DMA
    vmem = pltpu.VMEM
    gather_sems = [dma, dma((8,)), dma((2,)), dma((4, 2)), dma((4, 2)), dma, dma((8,))]
    return pl.pallas_call(
        layer_kernel,
        out_shape=jax.ShapeDtypeStruct((128, 56), BF),
        in_specs=[
            ANY, ANY, ANY, VM, VM, pl.BlockSpec(memory_space=pltpu.SMEM), ANY, ANY, VM, VM, VM,
            ANY, ANY, ANY,
        ],
        out_specs=VM,
        scratch_shapes=[
            vmem((64, 256), BF),
            vmem((2048, 256), BF),
            vmem((2048, 256), BF),
            vmem((128, 56), BF),
            vmem((56, 16384), BF),
            vmem((SLOTS, 7168), BF),
            vmem((SLOTS, 7168), BF),
            vmem((SLOTS, 7168), BF),
            vmem((336, 8192), BF),
            vmem((SLOTS, 8192), BF),
            vmem((8, 4, 2, 2, 128, 128), BF),
            vmem((8, 16, 16384), BF),
            vmem((2, 128, 128), BF),
            vmem((128, 128), BF),
            vmem((8, 4, 2, 2, 128, 128), BF),
            vmem((344, 256), F32),
            vmem((2, 2, 8, 2, SLOTS, 128), BF),
            vmem((2, 8, 2, SLOTS, 128), BF),
            vmem((16, 2, SLOTS, 128), BF),
            vmem((16, 2, SLOTS, 128), BF),
            vmem((2, 2, 128, 128), BF),
            vmem((8, 128, 128), BF),
            vmem((8, 256), F32),
            dma((8,)),
            *gather_sems,
            *gather_sems,
            dma, dma((2,)), dma, dma, dma, dma, dma, dma,
        ],
        compiler_params=pltpu.CompilerParams(
            collective_id=0, has_side_effects=True, vmem_limit_bytes=56 * 2**20
        ),
        name="decode_layer",
    )(
        queries, cache_keys, cache_values, new_keys, new_values, lengths, residual, out_weight,
        norm_gain.reshape(1, 7168), router_weight.T, routes.T, jnp.swapaxes(gate_tiles, 1, 2),
        jnp.swapaxes(up_tiles, 1, 2), down_tiles,
    )


def solution(mesh):
    return jax.shard_map(
        local,
        mesh=mesh,
        in_specs=(
            P(("pool", "rank"), None, None),
            P(("pool", "rank"), None, None),
            P(("pool", "rank"), None, None),
            P(("pool", "rank"), None),
            P(("pool", "rank"), None),
            P(("pool", "rank")),
            P("pool", "rank"),
            P("rank", None),
            P(),
            P(),
            P(),
            P(("pool", "rank"), None, None),
            P(("pool", "rank"), None, None),
            P(("pool", "rank"), None, None),
        ),
        out_specs=P("pool", "rank"),
        check_vma=False,
    )
```

time: 1100 us -> 116 us (0.11)
  the two profiles are of different devices: /device:TPU:8 before, /device:TPU:55 now
where the time goes in v2:
time: 116 us; the launch traced here: 115 us
  Pallas kernels  112 us (97%)
  local copies, waits for them, and re-layouts  2.86 us (2%)
    pallas_call x1, Pallas kernels, local(): pl.pallas_call(layer_kernel, out_shape=jax.ShapeDtypeStruct((128, 56), BF...  112 us

profile of v2, /device:TPU:55, one launch (start us, length us, event | category | flops | bytes accessed | tf_op | source)
XLA Modules:
  0.0 115.1 jit_solution(15256520484195312776)
XLA Ops:
  0.7 1.4 %copy.15.residual_hbm = bf16[128,56]{1,0:T(8,128)(2,1)} copy(bf16[128,56]{0,1:T(8,128)(2,1)} %param.20) | data formatting | bytes 28672 | tf_op args[6]
  2.1 111.5 %decode_layer.1 = bf16[128,56]{1,0:T(8,128)(2,1)} custom-call(bf16[1,64,256]{2,1,0:T(8,128)(2,1)} %queries_hbm.1, bf16[1,2048,256]{2,1,0:T(8,128)(2,1)} %keys_hbm.1, bf16[1,2048,256]{2,1,0:T(8,128)(2,1)} %values_hbm.1, bf16[1,256]{1,0:T(2,128)(2,1)} %new_key_ref.1, bf16[1,256]{1,0:T(2,128)(2,1)} %new_value_ref.1, s32[1]{0:T(128)S(6)} %copy.17.length_ref, ...), custom_call_target="tpu_custom_call" | custom-call | tf_op jit(solution)/shard_map/decode_layer/pallas_call | solution.py:423
  113.6 1.4 %copy.16 = bf16[128,56]{0,1:T(8,128)(2,1)} copy(bf16[128,56]{1,0:T(8,128)(2,1)} %decode_layer.1) | data formatting | bytes 28672 | tf_op jit(solution)/shard_map/decode_layer/pallas_call | solution.py:423

commit v3 on v2

--- a/solution.py
+++ b/solution.py
@@ -36,15 +36,20 @@
 
 
 def padded(tiles):
+    zeros = jnp.zeros((tiles[0].shape[0], 8), tiles[0].dtype)
     out = []
     for j in range(8):
         parts = []
-        if j > 0:
-            parts.append(tiles[j - 1][:, 128 - 16 * j :])
-        if j < 7:
-            parts.append(tiles[j][:, : WIDE - 16 * j])
-        parts.append(jnp.zeros((tiles[0].shape[0], 16), tiles[0].dtype))
-        out.append(jnp.concatenate([part for part in parts if part.shape[1]], axis=1))
+        for start in (WIDE * j, WIDE * j + 56):
+            while start % 56 or not parts or parts[-1] is zeros:
+                end = min(start // 56 * 56 + 56, start // 128 * 128 + 128)
+                base = start // 128 * 128
+                parts.append(tiles[start // 128][:, start - base : end - base])
+                start = end
+                if start % 56 == 0:
+                    break
+            parts.append(zeros)
+        out.append(jnp.concatenate(parts, axis=1))
     return out
 
 
@@ -55,10 +60,10 @@
 def layer_kernel(
     queries_hbm, keys_hbm, values_hbm, new_key_ref, new_value_ref, length_ref, residual_hbm,
     weight_hbm, gain_ref, router_ref, routes_ref, gate_hbm, up_hbm, down_hbm, out_ref,
-    queries, keys, values, residual, weight, gate, up, down, fused, cut, rows_in, rows, states_in,
-    state_sent, states, acc, partial, from_core, to_group, from_group, to_rows, from_experts,
+    queries, keys, values, residual, weight, gate, up, down, fused, cut, rows_in, rows, states,
+    acc, squares, partial, from_core, to_group, from_group, to_rows, from_experts,
     places, load_sem, a_plane, a_plane_in, a_ring, a_up_in, a_down_in, a_core, a_core_in, b_plane,
-    b_plane_in, b_ring, b_up_in, b_down_in, b_core, b_core_in, m_send, m_recv, c_send, c_recv,
+    b_plane_in, b_ring, b_up_in, b_down_in, b_core, b_core_in, c_send, c_recv,
     r_send, r_recv, d_send, d_recv,
 ):
     pool, rank = lax.axis_index("pool"), lax.axis_index("rank")
@@ -69,7 +74,6 @@
     sibling = rank + 1 - 2 * c
     up_rank = rank_of(lax.rem(z + 1, 8), x, yh, c)
     down_rank = rank_of(lax.rem(z + 7, 8), x, yh, c)
-    across = (pool == c).astype(jnp.int32)
     same = jnp.logical_and(z // 4 == zb, lax.rem(z // 2, 2) == c)
 
     def member(spot_of, core):
@@ -80,6 +84,9 @@
             src_ref=src, dst_ref=dst, send_sem=send, recv_sem=recv, device_id=(p, r),
             device_id_type=MESH,
         )
+
+    def in_plane(d):
+        return lax.rem(pool + d // 8, 2), z * 16 + lax.rem(x * 2 + yh + d, 8) * 2 + c
 
     def is_self(p, r):
         return jnp.logical_and(p == pool, r == rank)
@@ -102,24 +109,22 @@
             pl.semaphore_signal(barrier, inc=1, device_id=(p, r), device_id_type=MESH)
 
     def greet_plane(d, _):
-        greet(pool, z * 16 + lax.rem(x * 2 + yh + d, 8) * 2 + c)
+        greet(*in_plane(d))
         return 0
 
     def greet_group(d, _):
-        greet(pool, member(lax.rem(spot + d, 16), c))
+        greet(pool, member((1 - zb) * 8 + d, c))
         return 0
 
     def greet_sums(e, _):
         greet(e // 4, rank_of(2 * lax.rem(e, 4) + z // 4, x, yh, lax.rem(z // 2, 2)))
         return 0
 
-    lax.fori_loop(1, 8, greet_plane, 0)
+    lax.fori_loop(1, 16, greet_plane, 0)
     greet(pool, sibling)
     greet(pool, up_rank)
     greet(pool, down_rank)
-    for core in range(2):
-        greet(c, rank - c + core)
-    lax.fori_loop(1, 16, greet_group, 0)
+    lax.fori_loop(0, 8, greet_group, 0)
     lax.fori_loop(0, 8, greet_sums, 0)
 
     loads[0].wait()
@@ -144,29 +149,24 @@
     rows_in[z, x, yh, c, 0:64, :] = context[:, 0:128]
     rows_in[z, x, yh, c, 64:128, :] = context[:, 128:256]
 
-    pl.semaphore_wait(barrier, 35 - across - same.astype(jnp.int32))
-
-    def gather(buf, plane, plane_in, ring, up_in, down_in, core_send, core_in, work):
-        own = buf.at[z, x, yh, c]
-        flat = x * 2 + yh
+    pl.semaphore_wait(barrier, 34 - same.astype(jnp.int32))
+
+    def gather(count, own, block, chunk, whole, plane, plane_in, ring, up_in, down_in, core_send, core_in, work):
+        here = pool * 8 + x * 2 + yh
 
         def to_plane(d, _):
-            r = z * 16 + lax.rem(flat + d, 8) * 2 + c
-            copy(own, own, plane, plane_in.at[flat], pool, r).start()
+            p, r = in_plane(d)
+            copy(own, own, plane, plane_in.at[here], p, r).start()
             return 0
 
-        lax.fori_loop(1, 8, to_plane, 0)
-        work(-1)
-
         def landed(d, _):
-            j = lax.rem(flat + d, 8)
-            wait_bytes(buf.at[z, j // 2, lax.rem(j, 2), c], plane_in.at[j])
+            p, r = in_plane(d)
+            _, rx, ry, _ = place(r)
+            wait_bytes(block(p, rx, ry), plane_in.at[p * 8 + rx * 2 + ry])
             return 0
 
-        lax.fori_loop(1, 8, landed, 0)
-
-        def chunk(b, k):
-            return buf.at[b, pl.ds(2 * k, 2), :, c]
+        lax.fori_loop(1, count, to_plane, 0)
+        lax.fori_loop(1, count, landed, 0)
 
         def share(b, k):
             copy(chunk(b, k), chunk(b, k), core_send, core_in.at[b], pool, sibling).start()
@@ -187,14 +187,17 @@
                 if 0 < s < 4 or (s == 4 and k == 1):
                     share(b_down, k)
             work(s)
-        seven = buf.at[pl.ds(0, 7), pl.ds(0, 2), :, c]
-        wait_bytes(buf.at[pl.ds(0, 7), 0, 0, c], plane)
-        wait_bytes(seven, ring.at[0])
-        wait_bytes(seven, ring.at[1])
-        wait_bytes(buf.at[:, :, :, c], core_send)
-
-    def from_sibling(buf, core_in, b):
-        wait_bytes(buf.at[b, :, :, c], core_in.at[b])
+
+        def all_sent(d, _):
+            wait_bytes(own, plane)
+            return 0
+
+        lax.fori_loop(1, count, all_sent, 0)
+        for way in range(2):
+            for n in range(7):
+                wait_bytes(chunk(n, 0), ring.at[way])
+        for n in range(8):
+            wait_bytes(whole(n), core_send)
 
     def step_planes(s):
         if s in (0, 4):
@@ -235,40 +238,34 @@
         lax.fori_loop(0, 8, part, 0)
 
     def row_work(s):
-        if s < 0:
-            return
         if s == 0:
             for load in loads[5:]:
                 load.wait()
         if s < 4:
             lax.fori_loop(2 * s, 2 * s + 2, prepare, 0)
         for b in step_planes(s):
-            from_sibling(rows_in, a_core_in, b)
+            wait_bytes(row_plane(b), a_core_in.at[b])
             turn(b)
 
-    gather(rows_in, a_plane, a_plane_in, a_ring, a_up_in, a_down_in, a_core, a_core_in, row_work)
+    def row_plane(b):
+        return rows_in.at[b, :, :, c]
+
+    gather(
+        8, rows_in.at[z, x, yh, c], lambda p, rx, ry: rows_in.at[z, rx, ry, c],
+        lambda b, k: rows_in.at[b, pl.ds(2 * k, 2), :, c], row_plane, a_plane, a_plane_in, a_ring,
+        a_up_in, a_down_in, a_core, a_core_in, row_work,
+    )
 
     loads[3].wait()
     loads[4].wait()
     projected = lax.dot_general(
-        rows[...].reshape(128, 16384), weight[...], (((1,), (1,)), ((), ())),
+        weight[...], rows[...].reshape(128, 16384), (((1,), (1,)), ((), ())),
         preferred_element_type=F32,
     )
-    hstate = (residual[...].astype(F32) + projected).astype(BF)
-
-    shift = (iota((56, 128), 0) + 56 * c == iota((56, 128), 1)).astype(BF)
-    state_sent[...] = dot(hstate, shift).astype(BF)
-    for p in range(2):
-        r = rank - c + pool
-        here = is_self(p, r)
-
-        @pl.when(here)
-        def _():
-            pltpu.make_async_copy(state_sent, states_in.at[c], m_recv.at[c]).start()
-
-        @pl.when(jnp.logical_not(here))
-        def _():
-            copy(state_sent, states_in.at[c], m_send, m_recv.at[c], p, r).start()
+    hstate = (residual[...].astype(F32) + projected).astype(BF).astype(F32)
+    states[z, pool, x, yh, c] = jnp.concatenate(
+        [hstate, jnp.zeros((8, 128), F32)], axis=0
+    ).astype(BF)
 
     rows8 = iota((8, 256), 0)
     members = jnp.zeros((8, 256), F32)
@@ -277,43 +274,33 @@
     r0, r1 = iota((256, 256), 0), iota((256, 256), 1)
     order = dot(members.astype(BF), (r0 < r1).astype(BF))
     places[...] = jnp.where(members > 0.5, order, -1.0)
+    acc[...] = jnp.zeros_like(acc)
+    squares[...] = jnp.zeros_like(squares)
+
+    def state_work(s):
+        for b in step_planes(s):
+            wait_bytes(state_plane(b), b_core_in.at[b])
+            k = pl.ds(pl.multiple_of(b * 1024, 1024), 1024)
+            for p in range(2):
+                part = states[b, p].reshape(1024, 128)
+                lanes = slice(p * 128, p * 128 + 128)
+                acc[:, lanes] += dot(fused[:, k], part)
+                wide = part.astype(F32)
+                squares[:, lanes] += jnp.sum((wide * wide).reshape(128, 8, 128), axis=0)
+
+    def state_plane(b):
+        return states.at[b, :, :, :, c]
+
+    gather(
+        16, states.at[z, pool, x, yh, c], lambda p, rx, ry: states.at[z, p, rx, ry, c],
+        lambda b, k: states.at[b, k, :, :, c], state_plane, b_plane, b_plane_in, b_ring, b_up_in,
+        b_down_in, b_core, b_core_in, state_work,
+    )
+
     own_places = places[pl.ds(expert, 1), :]
     picked = own_places == iota((SLOTS, 256), 0).astype(F32)
     pick = picked.astype(BF)
-    acc[...] = jnp.zeros_like(acc)
-    for i in range(2):
-        wait_bytes(state_sent, m_recv.at[i])
-    states[z, x, yh, c] = states_in[0] + states_in[1]
-
-    def state_work(s):
-        if s < 0:
-            return
-        for b in step_planes(s):
-            from_sibling(states, b_core_in, b)
-            halves = []
-            for core in range(2):
-                halves.append(jnp.concatenate(
-                    [states[b, i // 2, i % 2, core] for i in range(8)], axis=1
-                ))
-            plane = jnp.concatenate(halves, axis=0)
-            wide = plane.astype(F32)
-            k = pl.ds(pl.multiple_of(b * 1024, 1024), 1024)
-            product = lax.dot_general(
-                fused[:, k], plane, (((1,), (1,)), ((), ())), preferred_element_type=F32
-            )
-            acc[0:336, :] += product
-            square = wide * wide
-            lanes = square[:, 0:128]
-            for i in range(1, 8):
-                lanes += square[:, i * 128 : i * 128 + 128]
-            acc[336:344, :] += lax.dot_general(
-                jnp.ones((8, 128), F32), lanes, (((1,), (1,)), ((), ())),
-                preferred_element_type=F32, precision=lax.Precision.HIGHEST,
-            )
-
-    gather(states, b_plane, b_plane_in, b_ring, b_up_in, b_down_in, b_core, b_core_in, state_work)
-
-    inv = lax.rsqrt(acc[336:337, :] * (1.0 / 7168) + EPSILON)
+    inv = lax.rsqrt(jnp.sum(squares[...], axis=0, keepdims=True) * (1.0 / 7168) + EPSILON)
     chosen = jax.nn.sigmoid(acc[320:328, :] * inv)
     named = jnp.where(members > 0.5, chosen, 0.0)
     whole = jnp.sum(named, axis=0, keepdims=True)
@@ -361,25 +348,22 @@
 
     lax.fori_loop(1, 16, send_sum, 0)
     from_group[spot] = chip_sum(spot)
-
-    column = lax.dot_general(
-        (r0 == r1).astype(BF), jnp.broadcast_to(own_places, (8, 256)).astype(BF),
-        (((1,), (1,)), ((), ())), preferred_element_type=F32,
-    )[:, 0:1]
-    spread_by = (column == iota((256, SLOTS), 1).astype(F32)).astype(BF)
     wait_bytes(from_group.at[pl.ds(0, 15)], r_recv)
 
     for i in range(2):
         total = from_group[0, i].astype(F32)
         for s in range(1, 16):
             total += from_group[s, i].astype(F32)
-        spread = dot(spread_by, total.astype(BF)).astype(BF)
+        spread = lax.dot_general(
+            total.astype(BF), pick, (((0,), (0,)), ((), ())), preferred_element_type=F32
+        ).astype(BF)
         for p in range(2):
-            to_rows[i, p] = spread[p * 128 : p * 128 + 128, :]
+            for core in range(2):
+                to_rows[i, p, core] = spread[core * 64 : core * 64 + 64, p * 128 : p * 128 + 128]
         for p in range(2):
             for core in range(2):
                 r = rank_of(4 * zb + 2 * c + i, x, yh, core)
-                src, dst = to_rows.at[i, p], from_experts.at[expert]
+                src, dst = to_rows.at[i, p, core], from_experts.at[expert]
                 here = is_self(p, r)
 
                 @pl.when(here)
@@ -394,15 +378,7 @@
     sums = from_experts[0].astype(F32)
     for e in range(1, 8):
         sums += from_experts[e].astype(F32)
-    back = (iota((128, 56), 0) == iota((128, 56), 1) + 56 * c).astype(F32)
-    mine_sum = jnp.dot(sums, back, preferred_element_type=F32, precision=lax.Precision.HIGHEST)
-    out_ref[...] = (hstate.astype(F32) + mine_sum).astype(BF)
-
-    wait_bytes(state_sent, m_send)
-
-    @pl.when(across == 0)
-    def _():
-        wait_bytes(state_sent, m_send)
+    out_ref[...] = (hstate + sums[0:56]).astype(BF)
 
     wait_bytes(from_core, c_send)
     wait_bytes(from_group.at[pl.ds(0, 15)], r_send)
@@ -419,10 +395,10 @@
 ):
     dma = pltpu.SemaphoreType.DMA
     vmem = pltpu.VMEM
-    gather_sems = [dma, dma((8,)), dma((2,)), dma((4, 2)), dma((4, 2)), dma, dma((8,))]
+    gather_sems = [dma, dma((16,)), dma((2,)), dma((4, 2)), dma((4, 2)), dma, dma((8,))]
     return pl.pallas_call(
         layer_kernel,
-        out_shape=jax.ShapeDtypeStruct((128, 56), BF),
+        out_shape=jax.ShapeDtypeStruct((56, 128), BF),
         in_specs=[
             ANY, ANY, ANY, VM, VM, pl.BlockSpec(memory_space=pltpu.SMEM), ANY, ANY, VM, VM, VM,
             ANY, ANY, ANY,
@@ -432,7 +408,7 @@
             vmem((64, 256), BF),
             vmem((2048, 256), BF),
             vmem((2048, 256), BF),
-            vmem((128, 56), BF),
+            vmem((56, 128), BF),
             vmem((56, 16384), BF),
             vmem((SLOTS, 7168), BF),
             vmem((SLOTS, 7168), BF),
@@ -441,31 +417,30 @@
             vmem((SLOTS, 8192), BF),
             vmem((8, 4, 2, 2, 128, 128), BF),
             vmem((8, 16, 16384), BF),
-            vmem((2, 128, 128), BF),
-            vmem((128, 128), BF),
-            vmem((8, 4, 2, 2, 128, 128), BF),
-            vmem((344, 256), F32),
+            vmem((8, 2, 4, 2, 2, 64, 128), BF),
+            vmem((336, 256), F32),
+            vmem((8, 256), F32),
             vmem((2, 2, 8, 2, SLOTS, 128), BF),
             vmem((2, 8, 2, SLOTS, 128), BF),
             vmem((16, 2, SLOTS, 128), BF),
             vmem((16, 2, SLOTS, 128), BF),
-            vmem((2, 2, 128, 128), BF),
-            vmem((8, 128, 128), BF),
+            vmem((2, 2, 2, 64, 128), BF),
+            vmem((8, 64, 128), BF),
             vmem((8, 256), F32),
             dma((8,)),
             *gather_sems,
             *gather_sems,
-            dma, dma((2,)), dma, dma, dma, dma, dma, dma,
+            dma, dma, dma, dma, dma, dma,
         ],
         compiler_params=pltpu.CompilerParams(
             collective_id=0, has_side_effects=True, vmem_limit_bytes=56 * 2**20
         ),
         name="decode_layer",
     )(
-        queries, cache_keys, cache_values, new_keys, new_values, lengths, residual, out_weight,
+        queries, cache_keys, cache_values, new_keys, new_values, lengths, residual.T, out_weight,
         norm_gain.reshape(1, 7168), router_weight.T, routes.T, jnp.swapaxes(gate_tiles, 1, 2),
         jnp.swapaxes(up_tiles, 1, 2), down_tiles,
-    )
+    ).T
 
 
 def solution(mesh):

time: 116 us -> 109 us (0.940)
  Pallas kernels: 112 us -> 106 us
  local copies, waits for them, and re-layouts: 2.86 us -> 1.31 us
    pallas_call x1, Pallas kernels: 112 us -> 106 us  [local(): pl.pallas_call(layer_kernel, out_shape=jax.ShapeDtypeStruct((56, 128), BF...]
    pallas_call x1 -> x0, local copies, waits for them, and re-layouts: 1.44 us -> none  [local(): pl.pallas_call(layer_kernel, out_shape=jax.ShapeDtypeStruct((128, 56), BF...]
where the time goes in v3:
time: 109 us; the launch traced here: 108 us
  Pallas kernels  106 us (97%)
  local copies, waits for them, and re-layouts  1.31 us (1%)
    pallas_call x1, Pallas kernels, local(): pl.pallas_call(layer_kernel, out_shape=jax.ShapeDtypeStruct((56, 128), BF...  106 us

profile of v3, /device:TPU:55, one launch (start us, length us, event | category | flops | bytes accessed | tf_op | source)
XLA Modules:
  0.0 108.4 jit_solution(14235862705000428088)
XLA Ops:
  0.7 106.5 %decode_layer.1 = bf16[56,128]{1,0:T(8,128)(2,1)} custom-call(bf16[1,64,256]{2,1,0:T(8,128)(2,1)} %queries_hbm.1, bf16[1,2048,256]{2,1,0:T(8,128)(2,1)} %keys_hbm.1, bf16[1,2048,256]{2,1,0:T(8,128)(2,1)} %values_hbm.1, bf16[1,256]{1,0:T(2,128)(2,1)} %new_key_ref.1, bf16[1,256]{1,0:T(2,128)(2,1)} %new_value_ref.1, s32[1]{0:T(128)S(6)} %copy.16.length_ref, ...), custom_call_target="tpu_custom_call" | custom-call | tf_op jit(solution)/shard_map/decode_layer/pallas_call | solution.py:399
  107.1 1.3 %copy.17 = bf16[128,56]{0,1:T(8,128)(2,1)} copy(bf16[128,56]{0,1:T(8,128)(2,1)} %bitcast.10) | data formatting | bytes 28672

commit v4 on v3

--- a/solution.py
+++ b/solution.py
@@ -62,9 +62,7 @@
     weight_hbm, gain_ref, router_ref, routes_ref, gate_hbm, up_hbm, down_hbm, out_ref,
     queries, keys, values, residual, weight, gate, up, down, fused, cut, rows_in, rows, states,
     acc, squares, partial, from_core, to_group, from_group, to_rows, from_experts,
-    places, load_sem, a_plane, a_plane_in, a_ring, a_up_in, a_down_in, a_core, a_core_in, b_plane,
-    b_plane_in, b_ring, b_up_in, b_down_in, b_core, b_core_in, c_send, c_recv,
-    r_send, r_recv, d_send, d_recv,
+    places, load_sem, c_send, c_recv, r_send, r_recv, d_send, d_recv, *gather_sems,
 ):
     pool, rank = lax.axis_index("pool"), lax.axis_index("rank")
     z, x, yh, c = place(rank)
@@ -72,8 +70,6 @@
     expert = pool * 4 + z // 2
     spot = zb * 8 + x * 2 + yh
     sibling = rank + 1 - 2 * c
-    up_rank = rank_of(lax.rem(z + 1, 8), x, yh, c)
-    down_rank = rank_of(lax.rem(z + 7, 8), x, yh, c)
     same = jnp.logical_and(z // 4 == zb, lax.rem(z // 2, 2) == c)
 
     def member(spot_of, core):
@@ -85,8 +81,8 @@
             device_id_type=MESH,
         )
 
-    def in_plane(d):
-        return lax.rem(pool + d // 8, 2), z * 16 + lax.rem(x * 2 + yh + d, 8) * 2 + c
+    def in_plane(d, core):
+        return lax.rem(pool + d // 8, 2), z * 16 + lax.rem(x * 2 + yh + d, 8) * 2 + core
 
     def is_self(p, r):
         return jnp.logical_and(p == pool, r == rank)
@@ -109,7 +105,13 @@
             pl.semaphore_signal(barrier, inc=1, device_id=(p, r), device_id_type=MESH)
 
     def greet_plane(d, _):
-        greet(*in_plane(d))
+        for core in range(2):
+            greet(*in_plane(d, core))
+        return 0
+
+    def greet_line(d, _):
+        for core in range(2):
+            greet(pool, rank_of(lax.rem(z + d, 8), x, yh, core))
         return 0
 
     def greet_group(d, _):
@@ -120,10 +122,29 @@
         greet(e // 4, rank_of(2 * lax.rem(e, 4) + z // 4, x, yh, lax.rem(z // 2, 2)))
         return 0
 
-    lax.fori_loop(1, 16, greet_plane, 0)
     greet(pool, sibling)
-    greet(pool, up_rank)
-    greet(pool, down_rank)
+
+    @pl.when(c == 0)
+    def _():
+        lax.fori_loop(1, 16, greet_plane, 0)
+        greet(pool, rank_of(lax.rem(z + 1, 8), x, yh, 0))
+        greet(pool, rank_of(lax.rem(z + 7, 8), x, yh, 0))
+
+    @pl.when(c == 1)
+    def _():
+        lax.fori_loop(1, 8, greet_line, 0)
+        for n in (1, 3):
+            greet(pool, rank_of(z, lax.rem(x + n, 4), yh, 1))
+        greet(pool, rank_of(z, x, 1 - yh, 1))
+        greet(1 - pool, rank)
+        greet(1 - pool, rank_of(z, x, 1 - yh, 1))
+
+        def greet_mates(d, _):
+            greet(pool, z * 16 + lax.rem(x * 2 + yh + d, 8) * 2 + 1)
+            return 0
+
+        lax.fori_loop(1, 8, greet_mates, 0)
+
     lax.fori_loop(0, 8, greet_group, 0)
     lax.fori_loop(0, 8, greet_sums, 0)
 
@@ -149,55 +170,191 @@
     rows_in[z, x, yh, c, 0:64, :] = context[:, 0:128]
     rows_in[z, x, yh, c, 64:128, :] = context[:, 128:256]
 
-    pl.semaphore_wait(barrier, 34 - same.astype(jnp.int32))
-
-    def gather(count, own, block, chunk, whole, plane, plane_in, ring, up_in, down_in, core_send, core_in, work):
-        here = pool * 8 + x * 2 + yh
+    pl.semaphore_wait(barrier, 41 + 10 * c - same.astype(jnp.int32))
+
+    def gather(buf, ny, w, device, sems, aside, work):
+        (
+            p_send, p_in, o_send, z_send, z_in, ring, up_in, down_in, y_send, y_in, x_send, l_in,
+            r_in, ll_in, rr_in, s_send, s_in,
+        ) = sems
+        half = buf.shape[4] // 2
+        first, second = pl.ds(0, half), pl.ds(half, half)
+        flat = x * ny + w
+        own = buf.at[z, x, w, c]
+
+        def put(ref, send, recv, to):
+            copy(ref, ref, send, recv, *to).start()
+
+        def near(n, core):
+            return device(lax.rem(z + n + 8, 8), x, w, core)
 
         def to_plane(d, _):
-            p, r = in_plane(d)
-            copy(own, own, plane, plane_in.at[here], p, r).start()
+            f = lax.rem(flat + d, 4 * ny)
+            put(own.at[first], p_send, p_in.at[flat * 2 + c], device(z, f // ny, lax.rem(f, ny), 0))
             return 0
 
-        def landed(d, _):
-            p, r = in_plane(d)
-            _, rx, ry, _ = place(r)
-            wait_bytes(block(p, rx, ry), plane_in.at[p * 8 + rx * 2 + ry])
+        @pl.when(c == 1)
+        def _():
+            put(own.at[first], o_send, p_in.at[flat * 2 + 1], device(z, x, w, 0))
+
+        @pl.when(c == 0)
+        def _():
+            put(own.at[second], o_send, z_in.at[z * 2], device(z, x, w, 1))
+
+        put(own.at[second], z_send, z_in.at[z * 2 + c], near(1, 1))
+        put(own.at[second], z_send, z_in.at[z * 2 + c], near(-1, 1))
+        lax.fori_loop(1, 4 * ny, to_plane, 0)
+        for n in (2, -2, 3, -3, 4):
+            put(own.at[second], z_send, z_in.at[z * 2 + c], near(n, 1))
+
+        def share(b, ref):
+            put(ref, s_send, s_in.at[b], device(z, x, w, 1 - c))
+
+        def share_near(core, rows):
+            for i in range(1, ny):
+                share(z, buf.at[z, x, lax.rem(w + i, ny), :, rows])
+            share(z, buf.at[z, x, w, core, rows])
+
+        def wait_plane(sem, rows, full):
+            blocks = buf.reshape(64 * ny, 2 * half, 128)
+            wait_bytes(blocks.at[pl.ds(0, 8 * ny if full else 8 * ny - 1), rows], sem)
+
+        def finish(n, rows):
+            for b in step_planes(n):
+                wait_plane(s_in.at[b], rows, n > 0)
+            work(step_planes(n))
+
+        @pl.when(c == 0)
+        def _():
+            def chunk(b, q):
+                return buf.at[b, lax.rem(x + (0, 1, 3, 2)[q], 4), :, :, first]
+
+            aside(0, 0)
+            for s in range(5):
+                b_up, b_down = lax.rem(z + 8 - s, 8), lax.rem(z + s, 8)
+                for q in range(4):
+                    up_now, down_now = s < 4 or q < 2, s < 4 or q >= 2
+                    if s == 0:
+                        xx = lax.rem(x + (0, 1, 3, 2)[q], 4)
+                        for i in range(ny):
+                            ww = lax.rem(w + i, ny)
+                            for core in range(2):
+                                if q or i or core:
+                                    wait_bytes(buf.at[z, xx, ww, core, first], p_in.at[(xx * ny + ww) * 2 + core])
+                    if s > 0 and up_now:
+                        wait_bytes(chunk(b_up, q), up_in.at[s - 1, q])
+                    if s < 3 or (s == 3 and q < 2):
+                        put(chunk(b_up, q), ring.at[0], up_in.at[s, q], near(1, 0))
+                    if s > 0 and down_now:
+                        wait_bytes(chunk(b_down, q), down_in.at[s - 1, q])
+                    if s < 3 or (s == 3 and q >= 2):
+                        put(chunk(b_down, q), ring.at[1], down_in.at[s, q], near(-1, 0))
+                    if s == 0 and q == 0:
+                        share_near(0, first)
+                    elif s == 0 or up_now:
+                        share(b_up, chunk(b_up, q))
+                    if s > 0 and down_now:
+                        share(b_down, chunk(b_down, q))
+                if s < 4:
+                    aside(0, s + 1)
+            for n in range(5):
+                finish(n, second)
+
+            def ring_sent(n, _):
+                for way in range(2):
+                    wait_bytes(chunk(n, 0), ring.at[way])
+                    wait_bytes(chunk(n, 0), ring.at[way])
+                return 0
+
+            lax.fori_loop(0, 7, ring_sent, 0)
+            for n in range(8):
+                wait_plane(s_send, first, n > 0)
+            wait_bytes(own.at[second], o_send)
+
+        @pl.when(c == 1)
+        def _():
+            left, right = device(z, lax.rem(x + 3, 4), w, 1), device(z, lax.rem(x + 1, 4), w, 1)
+            lx, rx, ox = lax.rem(x + 3, 4), lax.rem(x + 1, 4), lax.rem(x + 2, 4)
+
+            def along_z(n):
+                for b in step_planes(n):
+                    for core in range(2):
+                        if n or core == 0:
+                            wait_bytes(buf.at[b, x, w, core, second], z_in.at[b * 2 + core])
+                    line = buf.at[b, x, w, :, second]
+                    for i in range(1, ny):
+                        put(line, y_send, y_in.at[b], device(z, x, lax.rem(w + i, ny), 1))
+
+            def along_y(n):
+                for b in step_planes(n):
+                    wait_bytes(buf.at[b, x, pl.ds(0, ny - 1), :, second], y_in.at[b])
+                    face = buf.at[b, x, :, :, second]
+                    put(face, x_send, l_in.at[b], right)
+                    put(face, x_send, r_in.at[b], left)
+                    if n:
+                        share(b, face)
+                    else:
+                        share_near(1, second)
+
+            def along_x(n):
+                for b in step_planes(n):
+                    face = buf.at[b, lx, :, :, second]
+                    wait_bytes(face, l_in.at[b])
+                    put(buf.at[b, lx, pl.ds(0, ny // 2), :, second], x_send, ll_in.at[b], right)
+                    share(b, face)
+                    face = buf.at[b, rx, :, :, second]
+                    wait_bytes(face, r_in.at[b])
+                    put(buf.at[b, rx, pl.ds(ny // 2, ny // 2), :, second], x_send, rr_in.at[b], left)
+                    share(b, face)
+
+            def opposite(n):
+                for b in step_planes(n):
+                    wait_bytes(buf.at[b, ox, pl.ds(0, ny // 2), :, second], ll_in.at[b])
+                    wait_bytes(buf.at[b, ox, pl.ds(ny // 2, ny // 2), :, second], rr_in.at[b])
+                    share(b, buf.at[b, ox, :, :, second])
+
+            aside(1, 0)
+            along_z(0)
+            along_z(1)
+            along_y(0)
+            for n in (2, 3, 4):
+                along_z(n)
+            aside(1, 1)
+            along_y(1)
+            along_y(2)
+            aside(1, 2)
+            along_y(3)
+            along_y(4)
+            along_x(0)
+            along_x(1)
+            aside(1, 3)
+            for n in (2, 3, 4):
+                along_x(n)
+            for n in range(5):
+                opposite(n)
+            for n in range(5):
+                finish(n, first)
+
+            def line_sent(n, _):
+                wait_bytes(buf.at[n, x, pl.ds(0, ny - 1), :, second], y_send)
+                wait_bytes(buf.at[n, pl.ds(0, 3), :, :, second], x_send)
+                return 0
+
+            lax.fori_loop(0, 8, line_sent, 0)
+            for n in range(8):
+                wait_plane(s_send, second, n > 0)
+            wait_bytes(own.at[first], o_send)
+
+        def plane_sent(d, _):
+            wait_bytes(own.at[first], p_send)
             return 0
 
-        lax.fori_loop(1, count, to_plane, 0)
-        lax.fori_loop(1, count, landed, 0)
-
-        def share(b, k):
-            copy(chunk(b, k), chunk(b, k), core_send, core_in.at[b], pool, sibling).start()
-
-        for s in range(5):
-            b_up, b_down = lax.rem(z + 8 - s, 8), lax.rem(z + s, 8)
-            for k in range(2):
-                if s > 0 and (s < 4 or k == 0):
-                    wait_bytes(chunk(b_up, k), up_in.at[s - 1, k])
-                if s < 3 or (s == 3 and k == 0):
-                    copy(chunk(b_up, k), chunk(b_up, k), ring.at[0], up_in.at[s, k], pool, up_rank).start()
-                if s > 0 and (s < 4 or k == 1):
-                    wait_bytes(chunk(b_down, k), down_in.at[s - 1, k])
-                if s < 3 or (s == 3 and k == 1):
-                    copy(chunk(b_down, k), chunk(b_down, k), ring.at[1], down_in.at[s, k], pool, down_rank).start()
-                if s < 4 or k == 0:
-                    share(b_up, k)
-                if 0 < s < 4 or (s == 4 and k == 1):
-                    share(b_down, k)
-            work(s)
-
-        def all_sent(d, _):
-            wait_bytes(own, plane)
+        def line_sent(d, _):
+            wait_bytes(own.at[second], z_send)
             return 0
 
-        lax.fori_loop(1, count, all_sent, 0)
-        for way in range(2):
-            for n in range(7):
-                wait_bytes(chunk(n, 0), ring.at[way])
-        for n in range(8):
-            wait_bytes(whole(n), core_send)
+        lax.fori_loop(1, 4 * ny, plane_sent, 0)
+        lax.fori_loop(1, 8, line_sent, 0)
 
     def step_planes(s):
         if s in (0, 4):
@@ -237,24 +394,21 @@
 
         lax.fori_loop(0, 8, part, 0)
 
-    def row_work(s):
-        if s == 0:
+    def row_aside(core, n):
+        if n == 0:
             for load in loads[5:]:
                 load.wait()
-        if s < 4:
-            lax.fori_loop(2 * s, 2 * s + 2, prepare, 0)
-        for b in step_planes(s):
-            wait_bytes(row_plane(b), a_core_in.at[b])
+        bounds = ((0, 2, 3, 5, 7, 8), (0, 3, 5, 7, 8))[core]
+        lax.fori_loop(bounds[n], bounds[n + 1], prepare, 0)
+
+    def row_work(planes):
+        for b in planes:
             turn(b)
 
-    def row_plane(b):
-        return rows_in.at[b, :, :, c]
-
-    gather(
-        8, rows_in.at[z, x, yh, c], lambda p, rx, ry: rows_in.at[z, rx, ry, c],
-        lambda b, k: rows_in.at[b, pl.ds(2 * k, 2), :, c], row_plane, a_plane, a_plane_in, a_ring,
-        a_up_in, a_down_in, a_core, a_core_in, row_work,
-    )
+    def row_device(dz, dx, dw, core):
+        return pool, rank_of(dz, dx, dw, core)
+
+    gather(rows_in, 2, yh, row_device, gather_sems[:17], row_aside, row_work)
 
     loads[3].wait()
     loads[4].wait()
@@ -263,7 +417,7 @@
         preferred_element_type=F32,
     )
     hstate = (residual[...].astype(F32) + projected).astype(BF).astype(F32)
-    states[z, pool, x, yh, c] = jnp.concatenate(
+    states[z, x, yh * 2 + pool, c] = jnp.concatenate(
         [hstate, jnp.zeros((8, 128), F32)], axis=0
     ).astype(BF)
 
@@ -277,24 +431,23 @@
     acc[...] = jnp.zeros_like(acc)
     squares[...] = jnp.zeros_like(squares)
 
-    def state_work(s):
-        for b in step_planes(s):
-            wait_bytes(state_plane(b), b_core_in.at[b])
+    def state_work(planes):
+        for b in planes:
             k = pl.ds(pl.multiple_of(b * 1024, 1024), 1024)
             for p in range(2):
-                part = states[b, p].reshape(1024, 128)
+                part = jnp.concatenate(
+                    [states[b, n // 2, (n % 2) * 2 + p].reshape(128, 128) for n in range(8)], axis=0
+                )
                 lanes = slice(p * 128, p * 128 + 128)
                 acc[:, lanes] += dot(fused[:, k], part)
                 wide = part.astype(F32)
                 squares[:, lanes] += jnp.sum((wide * wide).reshape(128, 8, 128), axis=0)
 
-    def state_plane(b):
-        return states.at[b, :, :, :, c]
+    def state_device(dz, dx, dw, core):
+        return lax.rem(dw, 2), rank_of(dz, dx, dw // 2, core)
 
     gather(
-        16, states.at[z, pool, x, yh, c], lambda p, rx, ry: states.at[z, p, rx, ry, c],
-        lambda b, k: states.at[b, k, :, :, c], state_plane, b_plane, b_plane_in, b_ring, b_up_in,
-        b_down_in, b_core, b_core_in, state_work,
+        states, 4, yh * 2 + pool, state_device, gather_sems[17:], lambda core, n: None, state_work
     )
 
     own_places = places[pl.ds(expert, 1), :]
@@ -395,7 +548,13 @@
 ):
     dma = pltpu.SemaphoreType.DMA
     vmem = pltpu.VMEM
-    gather_sems = [dma, dma((16,)), dma((2,)), dma((4, 2)), dma((4, 2)), dma, dma((8,))]
+
+    def gather_sems(ny):
+        return [
+            dma, dma((8 * ny,)), dma, dma, dma((16,)), dma((2,)), dma((4, 4)), dma((4, 4)), dma,
+            dma((8,)), dma, dma((8,)), dma((8,)), dma((8,)), dma((8,)), dma, dma((8,)),
+        ]
+
     return pl.pallas_call(
         layer_kernel,
         out_shape=jax.ShapeDtypeStruct((56, 128), BF),
@@ -417,7 +576,7 @@
             vmem((SLOTS, 8192), BF),
             vmem((8, 4, 2, 2, 128, 128), BF),
             vmem((8, 16, 16384), BF),
-            vmem((8, 2, 4, 2, 2, 64, 128), BF),
+            vmem((8, 4, 4, 2, 64, 128), BF),
             vmem((336, 256), F32),
             vmem((8, 256), F32),
             vmem((2, 2, 8, 2, SLOTS, 128), BF),
@@ -428,9 +587,9 @@
             vmem((8, 64, 128), BF),
             vmem((8, 256), F32),
             dma((8,)),
-            *gather_sems,
-            *gather_sems,
             dma, dma, dma, dma, dma, dma,
+            *gather_sems(2),
+            *gather_sems(4),
         ],
         compiler_params=pltpu.CompilerParams(
             collective_id=0, has_side_effects=True, vmem_limit_bytes=56 * 2**20

time: 109 us -> 98.6 us (0.905)
  Pallas kernels: 106 us -> 96.5 us
    pallas_call x1, Pallas kernels: 106 us -> 96.5 us  [local(): pl.pallas_call(layer_kernel, out_shape=jax.ShapeDtypeStruct((56, 128), BF...]
where the time goes in v4:
time: 98.6 us; the launch traced here: 98.4 us
  Pallas kernels  96.5 us (98%)
  local copies, waits for them, and re-layouts  1.31 us (1%)
    pallas_call x1, Pallas kernels, local(): pl.pallas_call(layer_kernel, out_shape=jax.ShapeDtypeStruct((56, 128), BF...  96.5 us

profile of v4, /device:TPU:55, one launch (start us, length us, event | category | flops | bytes accessed | tf_op | source)
XLA Modules:
  0.0 98.4 jit_solution(7742052184979048768)
XLA Ops:
  0.7 96.5 %decode_layer.1 = bf16[56,128]{1,0:T(8,128)(2,1)} custom-call(bf16[1,64,256]{2,1,0:T(8,128)(2,1)} %queries_hbm.1, bf16[1,2048,256]{2,1,0:T(8,128)(2,1)} %keys_hbm.1, bf16[1,2048,256]{2,1,0:T(8,128)(2,1)} %values_hbm.1, bf16[1,256]{1,0:T(2,128)(2,1)} %new_key_ref.1, bf16[1,256]{1,0:T(2,128)(2,1)} %new_value_ref.1, s32[1]{0:T(128)S(6)} %copy.16.length_ref, ...), custom_call_target="tpu_custom_call" | custom-call | tf_op jit(solution)/shard_map/decode_layer/pallas_call | solution.py:558
  97.1 1.3 %copy.17 = bf16[128,56]{0,1:T(8,128)(2,1)} copy(bf16[128,56]{0,1:T(8,128)(2,1)} %bitcast.10) | data formatting | bytes 28672

commit v5 on v4

--- a/solution.py
+++ b/solution.py
@@ -58,9 +58,9 @@
 
 
 def layer_kernel(
-    queries_hbm, keys_hbm, values_hbm, new_key_ref, new_value_ref, length_ref, residual_hbm,
-    weight_hbm, gain_ref, router_ref, routes_ref, gate_hbm, up_hbm, down_hbm, out_ref,
-    queries, keys, values, residual, weight, gate, up, down, fused, cut, rows_in, rows, states,
+    queries_hbm, keys_hbm, values_hbm, new_key_hbm, new_value_hbm, length_hbm, residual_hbm,
+    weight_hbm, gain_hbm, router_hbm, routes_hbm, gate_hbm, up_hbm, down_hbm, out_ref,
+    new_key_ref, new_value_ref, length_ref, gain_ref, router_ref, routes_ref, queries, keys, values, residual, weight, gate, up, down, fused, cut, rows_in, rows, states,
     acc, squares, partial, from_core, to_group, from_group, to_rows, from_experts,
     places, load_sem, c_send, c_recv, r_send, r_recv, d_send, d_recv, *gather_sems,
 ):
@@ -87,15 +87,22 @@
     def is_self(p, r):
         return jnp.logical_and(p == pool, r == rank)
 
-    loads = []
-    for n, (src, dst) in enumerate((
-        (queries_hbm.at[0], queries), (keys_hbm.at[0], keys), (values_hbm.at[0], values),
-        (residual_hbm, residual), (weight_hbm, weight), (gate_hbm.at[0], gate),
-        (up_hbm.at[0], up), (down_hbm.at[0], down),
+    loads = {}
+    for n, (name, src, dst) in enumerate((
+        ("queries", queries_hbm.at[0], queries), ("keys", keys_hbm.at[0], keys),
+        ("new_key", new_key_hbm, new_key_ref), ("length", length_hbm, length_ref),
+        ("values", values_hbm.at[0], values), ("new_value", new_value_hbm, new_value_ref),
+        ("gain", gain_hbm, gain_ref), ("router", router_hbm, router_ref),
+        ("gate", gate_hbm.at[0], gate), ("up", up_hbm.at[0], up), ("down", down_hbm.at[0], down),
+        ("weight", weight_hbm, weight), ("residual", residual_hbm, residual),
+        ("routes", routes_hbm, routes_ref),
     )):
-        load = pltpu.make_async_copy(src, dst, load_sem.at[n])
-        load.start()
-        loads.append(load)
+        loads[name] = pltpu.make_async_copy(src, dst, load_sem.at[n])
+        loads[name].start()
+
+    def loaded(*names):
+        for name in names:
+            loads[name].wait()
 
     barrier = pltpu.get_barrier_semaphore()
 
@@ -112,14 +119,6 @@
     def greet_line(d, _):
         for core in range(2):
             greet(pool, rank_of(lax.rem(z + d, 8), x, yh, core))
-        return 0
-
-    def greet_group(d, _):
-        greet(pool, member((1 - zb) * 8 + d, c))
-        return 0
-
-    def greet_sums(e, _):
-        greet(e // 4, rank_of(2 * lax.rem(e, 4) + z // 4, x, yh, lax.rem(z // 2, 2)))
         return 0
 
     greet(pool, sibling)
@@ -139,17 +138,7 @@
         greet(1 - pool, rank)
         greet(1 - pool, rank_of(z, x, 1 - yh, 1))
 
-        def greet_mates(d, _):
-            greet(pool, z * 16 + lax.rem(x * 2 + yh + d, 8) * 2 + 1)
-            return 0
-
-        lax.fori_loop(1, 8, greet_mates, 0)
-
-    lax.fori_loop(0, 8, greet_group, 0)
-    lax.fori_loop(0, 8, greet_sums, 0)
-
-    loads[0].wait()
-    loads[1].wait()
+    loaded("queries", "keys", "new_key", "length")
     q = queries[...]
     scores = lax.dot_general(
         q, keys[...], (((1,), (1,)), ((), ())), preferred_element_type=F32
@@ -157,20 +146,20 @@
     self_score = jnp.sum(
         q.astype(F32) * new_key_ref[...].astype(F32), axis=1, keepdims=True
     ) * (1.0 / 16.0)
-    scores = jnp.where(iota((64, 2048), 1) < length_ref[0], scores, -1e30)
+    scores = jnp.where(iota((64, 2048), 1) < length_ref[...], scores, -1e30)
     highest = jnp.maximum(jnp.max(scores, axis=1, keepdims=True), self_score)
     raised = jnp.exp(scores - highest)
     raised_self = jnp.exp(self_score - highest)
     denominator = jnp.sum(raised, axis=1, keepdims=True) + raised_self
     weights = (raised / denominator).astype(BF)
     weight_self = (raised_self / denominator).astype(BF).astype(F32)
-    loads[2].wait()
+    loaded("values", "new_value")
     context = dot(weights, values[...]) + weight_self * new_value_ref[...].astype(F32)
     context = context.astype(BF)
     rows_in[z, x, yh, c, 0:64, :] = context[:, 0:128]
     rows_in[z, x, yh, c, 64:128, :] = context[:, 128:256]
 
-    pl.semaphore_wait(barrier, 41 + 10 * c - same.astype(jnp.int32))
+    pl.semaphore_wait(barrier, 25 + 3 * c)
 
     def gather(buf, ny, w, device, sems, aside, work):
         (
@@ -396,8 +385,7 @@
 
     def row_aside(core, n):
         if n == 0:
-            for load in loads[5:]:
-                load.wait()
+            loaded("gain", "router", "gate", "up", "down")
         bounds = ((0, 2, 3, 5, 7, 8), (0, 3, 5, 7, 8))[core]
         lax.fori_loop(bounds[n], bounds[n + 1], prepare, 0)
 
@@ -410,8 +398,7 @@
 
     gather(rows_in, 2, yh, row_device, gather_sems[:17], row_aside, row_work)
 
-    loads[3].wait()
-    loads[4].wait()
+    loaded("weight", "residual", "routes")
     projected = lax.dot_general(
         weight[...], rows[...].reshape(128, 16384), (((1,), (1,)), ((), ())),
         preferred_element_type=F32,
@@ -464,49 +451,58 @@
     ).astype(BF)
     share = jnp.sum(jnp.where(picked, row_share, 0.0), axis=1, keepdims=True)
 
-    def product(core, n):
-        b = 4 * (n // 2) + 2 * core + lax.rem(n, 2)
+    def product(core, g, i):
+        b = 4 * g + 2 * core + i
         k = pl.ds(pl.multiple_of(b * 1024, 1024), 1024)
         sums = (dot(hidden, cut[:, k]) * share).astype(BF)
         for j in range(8):
-            partial[core, n // 2, j, lax.rem(n, 2)] = sums[:, j * 128 : j * 128 + 128]
-
-    def other_half(n, _):
-        product(1 - c, n)
+            partial[core, i, g, j] = sums[:, j * 128 : j * 128 + 128]
+
+    def for_other(g, i):
+        product(1 - c, g, i)
         copy(
-            partial.at[1 - c, n // 2, :, lax.rem(n, 2)], from_core.at[n // 2, :, lax.rem(n, 2)],
-            c_send, c_recv, pool, sibling,
+            partial.at[1 - c, i, g], from_core.at[i, g], c_send, c_recv.at[2 * i + g], pool, sibling
         ).start()
-        return 0
-
-    def own_half(n, _):
-        product(c, n)
-        return 0
-
-    lax.fori_loop(0, 4, other_half, 0)
-    lax.fori_loop(0, 4, own_half, 0)
-    wait_bytes(from_core, c_recv)
-
-    def chip_sum(spot_of):
-        g, j = spot_of // 8, lax.rem(spot_of, 8)
-        return (partial[c, g, j].astype(F32) + from_core[g, j].astype(F32)).astype(BF)
-
-    def send_sum(d, _):
-        to = lax.rem(spot + d, 16)
-        to_group[to] = chip_sum(to)
-        copy(
-            to_group.at[to], from_group.at[spot], r_send, r_recv, pool, member(to, c)
-        ).start()
-        return 0
-
-    lax.fori_loop(1, 16, send_sum, 0)
-    from_group[spot] = chip_sum(spot)
-    wait_bytes(from_group.at[pl.ds(0, 15)], r_recv)
+
+    def send_sums(g, i):
+        wait_bytes(from_core.at[i, g], c_recv.at[2 * i + g])
+
+        def one(j, _):
+            to = g * 8 + j
+            both = (partial[c, i, g, j].astype(F32) + from_core[i, g, j].astype(F32)).astype(BF)
+
+            @pl.when(to == spot)
+            def _():
+                from_group[i, to] = both
+
+            @pl.when(to != spot)
+            def _():
+                to_group[i, to] = both
+                copy(
+                    to_group.at[i, to], from_group.at[i, spot], r_send, r_recv.at[i], pool,
+                    member(to, c),
+                ).start()
+
+            return 0
+
+        lax.fori_loop(0, 8, one, 0)
+
+    parts = ((0, 0), (1, 0), (0, 1), (1, 1))
+    for_other(*parts[0])
+    for_other(*parts[1])
+    product(c, *parts[0])
+    for n in range(4):
+        if n < 2:
+            for_other(*parts[n + 2])
+        if n < 3:
+            product(c, *parts[n + 1])
+        send_sums(*parts[n])
 
     for i in range(2):
-        total = from_group[0, i].astype(F32)
+        wait_bytes(from_group.at[i, pl.ds(0, 15)], r_recv.at[i])
+        total = from_group[i, 0].astype(F32)
         for s in range(1, 16):
-            total += from_group[s, i].astype(F32)
+            total += from_group[i, s].astype(F32)
         spread = lax.dot_general(
             total.astype(BF), pick, (((0,), (0,)), ((), ())), preferred_element_type=F32
         ).astype(BF)
@@ -534,7 +530,7 @@
     out_ref[...] = (hstate + sums[0:56]).astype(BF)
 
     wait_bytes(from_core, c_send)
-    wait_bytes(from_group.at[pl.ds(0, 15)], r_send)
+    wait_bytes(from_group.at[:, pl.ds(0, 15)], r_send)
     wait_bytes(from_experts.at[pl.ds(0, 7)], d_send)
 
     @pl.when(jnp.logical_not(same))
@@ -559,11 +555,16 @@
         layer_kernel,
         out_shape=jax.ShapeDtypeStruct((56, 128), BF),
         in_specs=[
-            ANY, ANY, ANY, VM, VM, pl.BlockSpec(memory_space=pltpu.SMEM), ANY, ANY, VM, VM, VM,
-            ANY, ANY, ANY,
+            ANY, ANY, ANY, ANY, ANY, ANY, ANY, ANY, ANY, ANY, ANY, ANY, ANY, ANY,
         ],
         out_specs=VM,
         scratch_shapes=[
+            vmem((1, 256), BF),
+            vmem((1, 256), BF),
+            vmem((1, 1), jnp.int32),
+            vmem((1, 7168), F32),
+            vmem((8, 7168), BF),
+            vmem((3, 256), jnp.int32),
             vmem((64, 256), BF),
             vmem((2048, 256), BF),
             vmem((2048, 256), BF),
@@ -579,15 +580,15 @@
             vmem((8, 4, 4, 2, 64, 128), BF),
             vmem((336, 256), F32),
             vmem((8, 256), F32),
-            vmem((2, 2, 8, 2, SLOTS, 128), BF),
-            vmem((2, 8, 2, SLOTS, 128), BF),
-            vmem((16, 2, SLOTS, 128), BF),
-            vmem((16, 2, SLOTS, 128), BF),
+            vmem((2, 2, 2, 8, SLOTS, 128), BF),
+            vmem((2, 2, 8, SLOTS, 128), BF),
+            vmem((2, 16, SLOTS, 128), BF),
+            vmem((2, 16, SLOTS, 128), BF),
             vmem((2, 2, 2, 64, 128), BF),
             vmem((8, 64, 128), BF),
             vmem((8, 256), F32),
-            dma((8,)),
-            dma, dma, dma, dma, dma, dma,
+            dma((14,)),
+            dma, dma((4,)), dma, dma((2,)), dma, dma,
             *gather_sems(2),
             *gather_sems(4),
         ],
@@ -596,7 +597,7 @@
         ),
         name="decode_layer",
     )(
-        queries, cache_keys, cache_values, new_keys, new_values, lengths, residual.T, out_weight,
+        queries, cache_keys, cache_values, new_keys, new_values, lengths.reshape(1, 1), residual.T, out_weight,
         norm_gain.reshape(1, 7168), router_weight.T, routes.T, jnp.swapaxes(gate_tiles, 1, 2),
         jnp.swapaxes(up_tiles, 1, 2), down_tiles,
     ).T

time: 98.6 us -> 92.2 us (0.935)
  Pallas kernels: 96.5 us -> 90 us
    pallas_call x1, Pallas kernels: 96.5 us -> 90 us  [local(): pl.pallas_call(layer_kernel, out_shape=jax.ShapeDtypeStruct((56, 128), BF...]
where the time goes in v5:
time: 92.2 us; the launch traced here: 92 us
  Pallas kernels  90 us (98%)
  local copies, waits for them, and re-layouts  1.31 us (1%)
    pallas_call x1, Pallas kernels, local(): pl.pallas_call(layer_kernel, out_shape=jax.ShapeDtypeStruct((56, 128), BF...  90 us

profile of v5, /device:TPU:55, one launch (start us, length us, event | category | flops | bytes accessed | tf_op | source)
XLA Modules:
  0.0 92.0 jit_solution(17190544439086203304)
XLA Ops:
  0.7 90.0 %decode_layer.1 = bf16[56,128]{1,0:T(8,128)(2,1)} custom-call(bf16[1,64,256]{2,1,0:T(8,128)(2,1)} %queries_hbm.1, bf16[1,2048,256]{2,1,0:T(8,128)(2,1)} %keys_hbm.1, bf16[1,2048,256]{2,1,0:T(8,128)(2,1)} %values_hbm.1, bf16[1,256]{1,0:T(2,128)(2,1)} %new_key_hbm.1, bf16[1,256]{1,0:T(2,128)(2,1)} %new_value_hbm.1, s32[1,1]{1,0:T(1,128)} %bitcast.8.length_hbm, ...), custom_call_target="tpu_custom_call" | custom-call | tf_op jit(solution)/shard_map/decode_layer/pallas_call | solution.py:554
  90.7 1.3 %copy.17 = bf16[128,56]{0,1:T(8,128)(2,1)} copy(bf16[128,56]{0,1:T(8,128)(2,1)} %bitcast.12) | data formatting | bytes 28672

commit v6 on v5

--- a/solution.py
+++ b/solution.py
@@ -61,7 +61,7 @@
     queries_hbm, keys_hbm, values_hbm, new_key_hbm, new_value_hbm, length_hbm, residual_hbm,
     weight_hbm, gain_hbm, router_hbm, routes_hbm, gate_hbm, up_hbm, down_hbm, out_ref,
     new_key_ref, new_value_ref, length_ref, gain_ref, router_ref, routes_ref, queries, keys, values, residual, weight, gate, up, down, fused, cut, rows_in, rows, states,
-    acc, squares, partial, from_core, to_group, from_group, to_rows, from_experts,
+    acc, squares, pick_ref, partial, from_core, to_group, from_group, to_rows, from_experts,
     places, load_sem, c_send, c_recv, r_send, r_recv, d_send, d_recv, *gather_sems,
 ):
     pool, rank = lax.axis_index("pool"), lax.axis_index("rank")
@@ -107,36 +107,28 @@
     barrier = pltpu.get_barrier_semaphore()
 
     def greet(p, r):
-        @pl.when(jnp.logical_not(is_self(p, r)))
-        def _():
-            pl.semaphore_signal(barrier, inc=1, device_id=(p, r), device_id_type=MESH)
-
-    def greet_plane(d, _):
-        for core in range(2):
-            greet(*in_plane(d, core))
-        return 0
-
-    def greet_line(d, _):
-        for core in range(2):
-            greet(pool, rank_of(lax.rem(z + d, 8), x, yh, core))
-        return 0
-
-    greet(pool, sibling)
+        pl.semaphore_signal(barrier, inc=1, device_id=(p, r), device_id_type=MESH)
 
     @pl.when(c == 0)
     def _():
-        lax.fori_loop(1, 16, greet_plane, 0)
-        greet(pool, rank_of(lax.rem(z + 1, 8), x, yh, 0))
-        greet(pool, rank_of(lax.rem(z + 7, 8), x, yh, 0))
+        for d in range(15, 0, -1):
+            for core in range(2):
+                greet(*in_plane(d, core))
+        for n in (1, 7):
+            greet(pool, rank_of(lax.rem(z + n, 8), x, yh, 0))
 
     @pl.when(c == 1)
     def _():
-        lax.fori_loop(1, 8, greet_line, 0)
+        for d in (4, 3, 5, 2, 6, 1, 7):
+            for core in range(2):
+                greet(pool, rank_of(lax.rem(z + d, 8), x, yh, core))
         for n in (1, 3):
             greet(pool, rank_of(z, lax.rem(x + n, 4), yh, 1))
         greet(pool, rank_of(z, x, 1 - yh, 1))
         greet(1 - pool, rank)
         greet(1 - pool, rank_of(z, x, 1 - yh, 1))
+
+    greet(pool, sibling)
 
     loaded("queries", "keys", "new_key", "length")
     q = queries[...]
@@ -159,15 +151,28 @@
     rows_in[z, x, yh, c, 0:64, :] = context[:, 0:128]
     rows_in[z, x, yh, c, 64:128, :] = context[:, 128:256]
 
+    loaded("routes")
+    rows8 = iota((8, 256), 0)
+    members = jnp.zeros((8, 256), F32)
+    for k in range(3):
+        members += (routes_ref[k : k + 1, :] == rows8).astype(F32)
+    r0, r1 = iota((256, 256), 0), iota((256, 256), 1)
+    order = dot(members.astype(BF), (r0 < r1).astype(BF))
+    places[...] = jnp.where(members > 0.5, order, -1.0)
+    acc[...] = jnp.zeros_like(acc)
+    squares[...] = jnp.zeros_like(squares)
+    own_places = places[pl.ds(expert, 1), :]
+    pick_ref[...] = (own_places == iota((SLOTS, 256), 0).astype(F32)).astype(BF)
+
     pl.semaphore_wait(barrier, 25 + 3 * c)
 
-    def gather(buf, ny, w, device, sems, aside, work):
+    def gather(buf, ny, w, part, device, sems, aside, work):
         (
             p_send, p_in, o_send, z_send, z_in, ring, up_in, down_in, y_send, y_in, x_send, l_in,
             r_in, ll_in, rr_in, s_send, s_in,
         ) = sems
-        half = buf.shape[4] // 2
-        first, second = pl.ds(0, half), pl.ds(half, half)
+        size = buf.shape[4]
+        first, second = pl.ds(0, part), pl.ds(part, size - part)
         flat = x * ny + w
         own = buf.at[z, x, w, c]
 
@@ -177,10 +182,9 @@
         def near(n, core):
             return device(lax.rem(z + n + 8, 8), x, w, core)
 
-        def to_plane(d, _):
+        def to_plane(d):
             f = lax.rem(flat + d, 4 * ny)
             put(own.at[first], p_send, p_in.at[flat * 2 + c], device(z, f // ny, lax.rem(f, ny), 0))
-            return 0
 
         @pl.when(c == 1)
         def _():
@@ -192,7 +196,8 @@
 
         put(own.at[second], z_send, z_in.at[z * 2 + c], near(1, 1))
         put(own.at[second], z_send, z_in.at[z * 2 + c], near(-1, 1))
-        lax.fori_loop(1, 4 * ny, to_plane, 0)
+        for d in range(1, 4 * ny):
+            to_plane(d)
         for n in (2, -2, 3, -3, 4):
             put(own.at[second], z_send, z_in.at[z * 2 + c], near(n, 1))
 
@@ -205,7 +210,7 @@
             share(z, buf.at[z, x, w, core, rows])
 
         def wait_plane(sem, rows, full):
-            blocks = buf.reshape(64 * ny, 2 * half, 128)
+            blocks = buf.reshape(64 * ny, size, 128)
             wait_bytes(blocks.at[pl.ds(0, 8 * ny if full else 8 * ny - 1), rows], sem)
 
         def finish(n, rows):
@@ -396,9 +401,9 @@
     def row_device(dz, dx, dw, core):
         return pool, rank_of(dz, dx, dw, core)
 
-    gather(rows_in, 2, yh, row_device, gather_sems[:17], row_aside, row_work)
-
-    loaded("weight", "residual", "routes")
+    gather(rows_in, 2, yh, 48, row_device, gather_sems[:17], row_aside, row_work)
+
+    loaded("weight", "residual")
     projected = lax.dot_general(
         weight[...], rows[...].reshape(128, 16384), (((1,), (1,)), ((), ())),
         preferred_element_type=F32,
@@ -407,16 +412,6 @@
     states[z, x, yh * 2 + pool, c] = jnp.concatenate(
         [hstate, jnp.zeros((8, 128), F32)], axis=0
     ).astype(BF)
-
-    rows8 = iota((8, 256), 0)
-    members = jnp.zeros((8, 256), F32)
-    for k in range(3):
-        members += (routes_ref[k : k + 1, :] == rows8).astype(F32)
-    r0, r1 = iota((256, 256), 0), iota((256, 256), 1)
-    order = dot(members.astype(BF), (r0 < r1).astype(BF))
-    places[...] = jnp.where(members > 0.5, order, -1.0)
-    acc[...] = jnp.zeros_like(acc)
-    squares[...] = jnp.zeros_like(squares)
 
     def state_work(planes):
         for b in planes:
@@ -434,12 +429,11 @@
         return lax.rem(dw, 2), rank_of(dz, dx, dw // 2, core)
 
     gather(
-        states, 4, yh * 2 + pool, state_device, gather_sems[17:], lambda core, n: None, state_work
+        states, 4, yh * 2 + pool, 32, state_device, gather_sems[17:], lambda core, n: None, state_work
     )
 
-    own_places = places[pl.ds(expert, 1), :]
-    picked = own_places == iota((SLOTS, 256), 0).astype(F32)
-    pick = picked.astype(BF)
+    pick = pick_ref[...]
+    members = (places[...] >= 0.0).astype(F32)
     inv = lax.rsqrt(jnp.sum(squares[...], axis=0, keepdims=True) * (1.0 / 7168) + EPSILON)
     chosen = jax.nn.sigmoid(acc[320:328, :] * inv)
     named = jnp.where(members > 0.5, chosen, 0.0)
@@ -449,7 +443,7 @@
     hidden = lax.dot_general(
         pick, hidden_t, (((1,), (1,)), ((), ())), preferred_element_type=F32
     ).astype(BF)
-    share = jnp.sum(jnp.where(picked, row_share, 0.0), axis=1, keepdims=True)
+    share = jnp.sum(jnp.where(pick.astype(F32) > 0.5, row_share, 0.0), axis=1, keepdims=True)
 
     def product(core, g, i):
         b = 4 * g + 2 * core + i
@@ -580,6 +574,7 @@
             vmem((8, 4, 4, 2, 64, 128), BF),
             vmem((336, 256), F32),
             vmem((8, 256), F32),
+            vmem((SLOTS, 256), BF),
             vmem((2, 2, 2, 8, SLOTS, 128), BF),
             vmem((2, 2, 8, SLOTS, 128), BF),
             vmem((2, 16, SLOTS, 128), BF),

time: 92.2 us -> 91.2 us (0.989)
    pallas_call x1, Pallas kernels: 90 us -> 89.1 us  [local(): pl.pallas_call(layer_kernel, out_shape=jax.ShapeDtypeStruct((56, 128), BF...]
where the time goes in v6:
time: 91.2 us; the launch traced here: 91 us
  Pallas kernels  89.1 us (98%)
  local copies, waits for them, and re-layouts  1.31 us (1%)
    pallas_call x1, Pallas kernels, local(): pl.pallas_call(layer_kernel, out_shape=jax.ShapeDtypeStruct((56, 128), BF...  89.1 us

profile of v6, /device:TPU:55, one launch (start us, length us, event | category | flops | bytes accessed | tf_op | source)
XLA Modules:
  0.0 91.0 jit_solution(9290109019144415318)
XLA Ops:
  0.7 89.1 %decode_layer.1 = bf16[56,128]{1,0:T(8,128)(2,1)} custom-call(bf16[1,64,256]{2,1,0:T(8,128)(2,1)} %queries_hbm.1, bf16[1,2048,256]{2,1,0:T(8,128)(2,1)} %keys_hbm.1, bf16[1,2048,256]{2,1,0:T(8,128)(2,1)} %values_hbm.1, bf16[1,256]{1,0:T(2,128)(2,1)} %new_key_hbm.1, bf16[1,256]{1,0:T(2,128)(2,1)} %new_value_hbm.1, s32[1,1]{1,0:T(1,128)} %bitcast.8.length_hbm, ...), custom_call_target="tpu_custom_call" | custom-call | tf_op jit(solution)/shard_map/decode_layer/pallas_call | solution.py:548
  89.7 1.3 %copy.17 = bf16[128,56]{0,1:T(8,128)(2,1)} copy(bf16[128,56]{0,1:T(8,128)(2,1)} %bitcast.12) | data formatting | bytes 28672

commit v7 on v6

--- a/solution.py
+++ b/solution.py
@@ -163,8 +163,6 @@
     squares[...] = jnp.zeros_like(squares)
     own_places = places[pl.ds(expert, 1), :]
     pick_ref[...] = (own_places == iota((SLOTS, 256), 0).astype(F32)).astype(BF)
-
-    pl.semaphore_wait(barrier, 25 + 3 * c)
 
     def gather(buf, ny, w, part, device, sems, aside, work):
         (
@@ -251,7 +249,9 @@
                         share(b_down, chunk(b_down, q))
                 if s < 4:
                     aside(0, s + 1)
-            for n in range(5):
+                if s == 3:
+                    finish(0, second)
+            for n in range(1, 5):
                 finish(n, second)
 
             def ring_sent(n, _):
@@ -324,10 +324,11 @@
             aside(1, 3)
             for n in (2, 3, 4):
                 along_x(n)
-            for n in range(5):
+            opposite(0)
+            for n in range(1, 5):
                 opposite(n)
-            for n in range(5):
-                finish(n, first)
+                finish(n - 1, first)
+            finish(4, first)
 
             def line_sent(n, _):
                 wait_bytes(buf.at[n, x, pl.ds(0, ny - 1), :, second], y_send)
@@ -369,6 +370,14 @@
                 to = pl.ds(pl.multiple_of(first + n * 32, 32), 32)
                 for j in range(8):
                     fused[to, lane_tile(b * 8 + j)] = (tiles[j].astype(F32) * gains[j]).astype(BF)
+            return 0
+
+        lax.fori_loop(0, 5, strip, 0)
+        return 0
+
+    def prepare_down(b, _):
+        def strip(n, _):
+            r = pl.ds(pl.multiple_of(n * 32, 32), 32)
             tiles = padded([down[r, lane_tile(b * 7 + j)] for j in range(7)])
             for j in range(8):
                 cut[r, lane_tile(b * 8 + j)] = tiles[j]
@@ -389,10 +398,10 @@
         lax.fori_loop(0, 8, part, 0)
 
     def row_aside(core, n):
-        if n == 0:
-            loaded("gain", "router", "gate", "up", "down")
-        bounds = ((0, 2, 3, 5, 7, 8), (0, 3, 5, 7, 8))[core]
-        lax.fori_loop(bounds[n], bounds[n + 1], prepare, 0)
+        first = (2, 2)[core] if n == 0 else ((4, 5, 6, 7), (5, 8, 8))[core][n - 1]
+        last = ((4, 5, 6, 7, 8), (5, 8, 8, 8))[core][n]
+        if first < last:
+            lax.fori_loop(first, last, prepare, 0)
 
     def row_work(planes):
         for b in planes:
@@ -401,6 +410,9 @@
     def row_device(dz, dx, dw, core):
         return pool, rank_of(dz, dx, dw, core)
 
+    loaded("gain", "router", "gate", "up")
+    lax.fori_loop(0, 2, prepare, 0)
+    pl.semaphore_wait(barrier, 25 + 3 * c)
     gather(rows_in, 2, yh, 48, row_device, gather_sems[:17], row_aside, row_work)
 
     loaded("weight", "residual")
@@ -425,11 +437,19 @@
                 wide = part.astype(F32)
                 squares[:, lanes] += jnp.sum((wide * wide).reshape(128, 8, 128), axis=0)
 
+    def state_aside(core, n):
+        if n == 0:
+            loaded("down")
+        first = 0 if n == 0 else ((3, 5, 6, 7), (4, 8, 8))[core][n - 1]
+        last = ((3, 5, 6, 7, 8), (4, 8, 8, 8))[core][n]
+        if first < last:
+            lax.fori_loop(first, last, prepare_down, 0)
+
     def state_device(dz, dx, dw, core):
         return lax.rem(dw, 2), rank_of(dz, dx, dw // 2, core)
 
     gather(
-        states, 4, yh * 2 + pool, 32, state_device, gather_sems[17:], lambda core, n: None, state_work
+        states, 4, yh * 2 + pool, 32, state_device, gather_sems[17:], state_aside, state_work
     )
 
     pick = pick_ref[...]

time: 91.2 us -> 91.9 us (level)
  no operation moved by 1% of the time
where the time goes in v7:
time: 91.9 us; the launch traced here: 91.7 us
  Pallas kernels  89.7 us (98%)
  local copies, waits for them, and re-layouts  1.31 us (1%)
    pallas_call x1, Pallas kernels, local(): pl.pallas_call(layer_kernel, out_shape=jax.ShapeDtypeStruct((56, 128), BF...  89.7 us

profile of v7, /device:TPU:55, one launch (start us, length us, event | category | flops | bytes accessed | tf_op | source)
XLA Modules:
  0.0 91.7 jit_solution(13154568564945140277)
XLA Ops:
  0.7 89.7 %decode_layer.1 = bf16[56,128]{1,0:T(8,128)(2,1)} custom-call(bf16[1,64,256]{2,1,0:T(8,128)(2,1)} %queries_hbm.1, bf16[1,2048,256]{2,1,0:T(8,128)(2,1)} %keys_hbm.1, bf16[1,2048,256]{2,1,0:T(8,128)(2,1)} %values_hbm.1, bf16[1,256]{1,0:T(2,128)(2,1)} %new_key_hbm.1, bf16[1,256]{1,0:T(2,128)(2,1)} %new_value_hbm.1, s32[1,1]{1,0:T(1,128)} %bitcast.8.length_hbm, ...), custom_call_target="tpu_custom_call" | custom-call | tf_op jit(solution)/shard_map/decode_layer/pallas_call | solution.py:568
  90.3 1.3 %copy.17 = bf16[128,56]{0,1:T(8,128)(2,1)} copy(bf16[128,56]{0,1:T(8,128)(2,1)} %bitcast.12) | data formatting | bytes 28672

commit v8 on v6

--- a/solution.py
+++ b/solution.py
@@ -166,7 +166,7 @@
 
     pl.semaphore_wait(barrier, 25 + 3 * c)
 
-    def gather(buf, ny, w, part, device, sems, aside, work):
+    def gather(buf, ny, w, part, device, sems, aside, work, mixed):
         (
             p_send, p_in, o_send, z_send, z_in, ring, up_in, down_in, y_send, y_in, x_send, l_in,
             r_in, ll_in, rr_in, s_send, s_in,
@@ -194,12 +194,10 @@
         def _():
             put(own.at[second], o_send, z_in.at[z * 2], device(z, x, w, 1))
 
-        put(own.at[second], z_send, z_in.at[z * 2 + c], near(1, 1))
-        put(own.at[second], z_send, z_in.at[z * 2 + c], near(-1, 1))
+        for n in (1, -1, 2, -2, 3, -3, 4):
+            put(own.at[second], z_send, z_in.at[z * 2 + c], near(n, 1))
         for d in range(1, 4 * ny):
             to_plane(d)
-        for n in (2, -2, 3, -3, 4):
-            put(own.at[second], z_send, z_in.at[z * 2 + c], near(n, 1))
 
         def share(b, ref):
             put(ref, s_send, s_in.at[b], device(z, x, w, 1 - c))
@@ -251,7 +249,9 @@
                         share(b_down, chunk(b_down, q))
                 if s < 4:
                     aside(0, s + 1)
-            for n in range(5):
+                if s == 3 and mixed:
+                    finish(0, second)
+            for n in range(1 if mixed else 0, 5):
                 finish(n, second)
 
             def ring_sent(n, _):
@@ -295,11 +295,11 @@
                     face = buf.at[b, lx, :, :, second]
                     wait_bytes(face, l_in.at[b])
                     put(buf.at[b, lx, pl.ds(0, ny // 2), :, second], x_send, ll_in.at[b], right)
-                    share(b, face)
-                    face = buf.at[b, rx, :, :, second]
-                    wait_bytes(face, r_in.at[b])
+                    other = buf.at[b, rx, :, :, second]
+                    wait_bytes(other, r_in.at[b])
                     put(buf.at[b, rx, pl.ds(ny // 2, ny // 2), :, second], x_send, rr_in.at[b], left)
                     share(b, face)
+                    share(b, other)
 
             def opposite(n):
                 for b in step_planes(n):
@@ -326,7 +326,9 @@
                 along_x(n)
             for n in range(5):
                 opposite(n)
-            for n in range(5):
+                if mixed and n:
+                    finish(n - 1, first)
+            for n in range(4 if mixed else 0, 5):
                 finish(n, first)
 
             def line_sent(n, _):
@@ -401,7 +403,7 @@
     def row_device(dz, dx, dw, core):
         return pool, rank_of(dz, dx, dw, core)
 
-    gather(rows_in, 2, yh, 48, row_device, gather_sems[:17], row_aside, row_work)
+    gather(rows_in, 2, yh, 48, row_device, gather_sems[:17], row_aside, row_work, False)
 
     loaded("weight", "residual")
     projected = lax.dot_general(
@@ -429,7 +431,8 @@
         return lax.rem(dw, 2), rank_of(dz, dx, dw // 2, core)
 
     gather(
-        states, 4, yh * 2 + pool, 32, state_device, gather_sems[17:], lambda core, n: None, state_work
+        states, 4, yh * 2 + pool, 16, state_device, gather_sems[17:], lambda core, n: None, state_work,
+        True,
     )
 
     pick = pick_ref[...]

time: 91.2 us -> 89.3 us (0.979)
  Pallas kernels: 89.1 us -> 87.1 us
    pallas_call x1, Pallas kernels: 89.1 us -> 87.1 us  [local(): pl.pallas_call(layer_kernel, out_shape=jax.ShapeDtypeStruct((56, 128), BF...]
where the time goes in v8:
time: 89.3 us; the launch traced here: 89.1 us
  Pallas kernels  87.1 us (98%)
  local copies, waits for them, and re-layouts  1.31 us (1%)
    pallas_call x1, Pallas kernels, local(): pl.pallas_call(layer_kernel, out_shape=jax.ShapeDtypeStruct((56, 128), BF...  87.1 us

profile of v8, /device:TPU:55, one launch (start us, length us, event | category | flops | bytes accessed | tf_op | source)
XLA Modules:
  0.0 89.1 jit_solution(2966424882144952509)
XLA Ops:
  0.7 87.1 %decode_layer.1 = bf16[56,128]{1,0:T(8,128)(2,1)} custom-call(bf16[1,64,256]{2,1,0:T(8,128)(2,1)} %queries_hbm.1, bf16[1,2048,256]{2,1,0:T(8,128)(2,1)} %keys_hbm.1, bf16[1,2048,256]{2,1,0:T(8,128)(2,1)} %values_hbm.1, bf16[1,256]{1,0:T(2,128)(2,1)} %new_key_hbm.1, bf16[1,256]{1,0:T(2,128)(2,1)} %new_value_hbm.1, s32[1,1]{1,0:T(1,128)} %bitcast.8.length_hbm, ...), custom_call_target="tpu_custom_call" | custom-call | tf_op jit(solution)/shard_map/decode_layer/pallas_call | solution.py:551
  87.8 1.3 %copy.17 = bf16[128,56]{0,1:T(8,128)(2,1)} copy(bf16[128,56]{0,1:T(8,128)(2,1)} %bitcast.12) | data formatting | bytes 28672
